TPU v7x, 128 devices: a whole 4x4x4 slice. The times are simulated.
128 devices in a mesh: dp: 8 (over z_hi, y), vocab: 16 (over x, z_lo, core).
Axes of the slice: x: 4, y: 4, z: 4 (z_hi: 2, z_lo: 2; z = z_hi * 2 + z_lo), core: 2. Of those that a mesh axis runs over, the one named last changes fastest.
Arguments:
- start_hidden: bfloat16 [512, 3072], P('dp'), may hold values from -10.464474 to 10.464474
- offsets: bfloat16 [512, 3072], P('dp'), may hold values from -1.8042196 to 1.8042196
- norm_gain: float32 [3072], replicated, may hold values from 0.5 to 1.5
- head_table: bfloat16 [131072, 3072], P(('dp', 'vocab')), may hold values from -0.3969283 to 0.3969283
- targets_one: int32 [512], replicated, may hold values from 0 to 131071
- targets_two: int32 [512], replicated, may hold values from 0 to 131071
- advantage: int32 [512], replicated, may hold values from -2 to 2
Outputs:
- head_grad: float32 [131072, 3072], P(('dp', 'vocab'))
- gain_grad: float32 [3072], replicated
- offset_grad: bfloat16 [512, 3072], P('dp')
All inputs are finite; a program needn't handle non-finite values.
Results may differ from a plain program's by a relative error of at most 0.009.
Values may be sent and summed in bfloat16 or wider, within the bound.
No kernel may reach another device: no remote copies, remote signals or barrier semaphores. Data moves between devices by JAX's collectives and lax.ppermute only.
A program may use at most 128 MiB of HBM per device.

v0:
```python
import functools

import jax
import jax.numpy as jnp
from jax import lax
from jax.experimental import pallas as pl
from jax.experimental.pallas import tpu as pltpu
from jax.sharding import Mesh, PartitionSpec as P

ENTROPY_WEIGHT = 0.05
NORM_EPS = 1e-05
DP = ("zh", "y")
VOCAB = ("x", "zl", "c")
CHIPS = ("zh", "y", "x", "zl")
SWAP = [(0, 1), (1, 0)]
VOCAB_TILE = 256
WIDTH_TILE = 512
LANES = 128
f32 = jnp.float32
bf16 = jnp.bfloat16


def swap(value):
    return lax.ppermute(value, "c", SWAP)


def exchange(blocks, axes):
    return lax.all_to_all(blocks, axes, 0, 0)


def spread(piece, axes):
    n = lax.axis_size(axes)
    return exchange(jnp.broadcast_to(piece[None], (n,) + piece.shape), axes)


def whole():
    return pl.BlockSpec(memory_space=pltpu.VMEM)


def in_vmem(value):
    return pltpu.with_memory_space_constraint(value, pltpu.VMEM)


def call(kernel, operands, out_shape, scratch_shapes=(), scalars=0, vmem=16, far=()):
    specs = [pl.BlockSpec(memory_space=pltpu.SMEM)] * scalars
    specs += [whole()] * (len(operands) - scalars)
    for k in far:
        specs[k] = pl.BlockSpec(memory_space=pl.ANY)
    return pl.pallas_call(
        kernel,
        in_specs=specs,
        out_shape=out_shape,
        out_specs=[whole()] * len(out_shape),
        scratch_shapes=scratch_shapes,
        compiler_params=pltpu.CompilerParams(vmem_limit_bytes=vmem * 1024 * 1024),
    )(*operands)


def gather_rows(pieces_ref, rows_ref):
    width = rows_ref.shape[1]
    for j in range(rows_ref.shape[0] // 16):
        part = [pieces_ref[4 * j + k, :, :width].astype(f32) for k in range(4)]
        rows_ref[16 * j : 16 * j + 16, :] = jnp.concatenate(part, axis=0).astype(bf16)


def scatter_rows(value, pieces_ref, start):
    for j in range(value.shape[0] // 4):
        pieces_ref[j, :, start : start + value.shape[1]] = value[4 * j : 4 * j + 4].astype(bf16)


def nt(left, right):
    return lax.dot_general(left, right, (((1,), (1,)), ((), ())), preferred_element_type=f32)


def together(*values):
    return lax.optimization_barrier(values)


def logits_kernel(second, *refs):
    if second:
        pieces, own, other, logits, stats, hidden = refs
        gather_rows(pieces, hidden)
    else:
        hidden, far_own, far_other, logits, stats, own, other, sems = refs
        steps = own.shape[0] // VOCAB_TILE
        copies = [
            pltpu.make_async_copy(
                far.at[pl.ds(k * VOCAB_TILE, VOCAB_TILE)],
                near.at[pl.ds(k * VOCAB_TILE, VOCAB_TILE)],
                sems.at[t * steps + k],
            )
            for t, (far, near) in enumerate(((far_own, own), (far_other, other)))
            for k in range(steps)
        ]
        for copy in copies:
            copy.start()
    n_rows = logits.shape[1]
    block = other.shape[0]
    old = jnp.full((1, n_rows), -1e30, f32)
    total = jnp.zeros((1, n_rows), f32)
    weighted = total
    for table, base in ((own, 0), (other, block)):
        for start in range(0, block, VOCAB_TILE):
            if not second:
                copies[(base + start) // VOCAB_TILE].wait()
            tile = nt(table[start : start + VOCAB_TILE, :], hidden[...])
            logits[base + start : base + start + VOCAB_TILE, :] = tile
            top = jnp.maximum(old, jnp.max(tile, axis=0, keepdims=True))
            shifted = tile - top
            expo = jnp.exp(shifted)
            scale = jnp.exp(old - top)
            weighted = scale * (weighted + (old - top) * total) + jnp.sum(
                expo * shifted, axis=0, keepdims=True
            )
            total = scale * total + jnp.sum(expo, axis=0, keepdims=True)
            old = top
    lines = [v[:, k : k + LANES] for v in (old, total, weighted) for k in range(0, n_rows, LANES)]
    lines += [jnp.zeros((1, LANES), f32)] * (stats.shape[1] - len(lines))
    stats[...] = jnp.broadcast_to(jnp.concatenate(lines, axis=0)[None], stats.shape)


def logits_call(hidden, tables, n_chip):
    block, width = tables[0].shape
    second = hidden.ndim == 3
    rows = hidden.size // width
    out_shape = [
        pltpu.VMEM((2 * block, rows), f32),
        jax.ShapeDtypeStruct((n_chip, 8, LANES), f32),
    ]
    if second:
        out_shape.append(jax.ShapeDtypeStruct((rows, width), bf16))
        return call(
            functools.partial(logits_kernel, True),
            [hidden, in_vmem(tables[0]), in_vmem(tables[1])],
            out_shape,
        )
    out_shape += [pltpu.VMEM((block, width), bf16)] * 2
    return call(
        functools.partial(logits_kernel, False),
        [hidden] + [pltpu.with_memory_space_constraint(t, pltpu.HBM) for t in tables],
        out_shape,
        [pltpu.SemaphoreType.DMA((2 * block // VOCAB_TILE,))],
        far=(1, 2),
    )


def all_stats(stats, n_rows):
    n = n_rows // LANES
    top, total, weighted = (
        jnp.concatenate([stats[:, k * n + j, :] for j in range(n)], axis=1) for k in range(3)
    )
    peak = jnp.max(top, axis=0, keepdims=True)
    gap = top - peak
    scale = jnp.exp(gap)
    total_all = jnp.sum(scale * total, axis=0, keepdims=True)
    weighted_all = jnp.sum(scale * (weighted + gap * total), axis=0, keepdims=True)
    return peak + jnp.log(total_all), peak + weighted_all / total_all


def logit_grad(logits, probs, mean, adv, entries, targets):
    onehot = (entries == targets).astype(f32)
    return -adv * (onehot - probs) + ENTROPY_WEIGHT * probs * (logits - mean)


def entries_of(first, n, rows):
    return first + lax.broadcasted_iota(jnp.int32, (n, rows), 0)


def mixture_kernel(with_grad, *refs):
    if with_grad:
        first, logits, stats, targets, adv, own, other, hidden, gain = refs[:9]
    else:
        logits, stats, own, other = refs[:4]
    coef, partial, rows, turned = refs[-4:]
    block, width = own.shape
    n_rows = logits.shape[1]
    lse, mean = all_stats(stats, n_rows)
    rows[...] = jnp.concatenate([lse, mean] + [jnp.zeros_like(lse)] * 6, axis=0)
    for start in range(0, 2 * block, VOCAB_TILE):
        tile = logits[start : start + VOCAB_TILE, :]
        probs = jnp.exp(tile - lse)
        if with_grad:
            entry = first[start // block] + start % block
            entries = entries_of(entry, VOCAB_TILE, n_rows)
            probs = logit_grad(tile, probs, mean, adv[...], entries, targets[...])
        coef[start : start + VOCAB_TILE, :] = probs.astype(bf16)
        turned[:, start : start + VOCAB_TILE] = probs.T.astype(bf16)
    if with_grad:
        filled = width // LANES
        partial[filled:, :, width:] = jnp.zeros((partial.shape[0] - filled, 4, LANES), bf16)
    for start in range(0, width, WIDTH_TILE):
        columns = slice(start, start + WIDTH_TILE)
        value = jnp.dot(turned[:, :block], own[:, columns], preferred_element_type=f32)
        value = value + jnp.dot(turned[:, block:], other[:, columns], preferred_element_type=f32)
        scatter_rows(value, partial, start)
        if with_grad:
            unit = hidden[:, columns].astype(f32) / gain[:, columns]
            share = jnp.sum(unit * value, axis=0, keepdims=True)
            high = share.astype(bf16).astype(f32)
            middle = (share - high).astype(bf16).astype(f32)
            low = share - high - middle
            parts = jnp.concatenate([high, middle, low, jnp.zeros_like(low)], axis=0).astype(bf16)
            for k in range(WIDTH_TILE // LANES):
                piece = start // LANES + k
                partial[piece, :, width:] = parts[:, k * LANES : (k + 1) * LANES]


def mixture_call(logits, stats, tables, grad=None):
    block, width = tables[0].shape
    n_rows = logits.shape[1]
    tables = [in_vmem(t) for t in tables]
    operands = [in_vmem(logits), stats, *tables]
    out_width = width
    scalars = 0
    if grad is not None:
        first, targets, adv, hidden, gain = grad
        out_width += LANES
        operands = [first, in_vmem(logits), stats, targets, adv, *tables, hidden, gain]
        scalars = 1
    return call(
        functools.partial(mixture_kernel, grad is not None),
        operands,
        [
            jax.ShapeDtypeStruct((2 * block, n_rows), bf16),
            jax.ShapeDtypeStruct((n_rows // 4, 4, out_width), bf16),
            jax.ShapeDtypeStruct((8, n_rows), f32),
        ],
        [pltpu.VMEM((n_rows, 2 * block), bf16)],
        scalars,
    )


def in_thirds(value):
    high = value.astype(bf16).astype(f32)
    middle = (value - high).astype(bf16).astype(f32)
    return high, middle, value - high - middle


def sum_pieces(parts):
    total = parts[0].astype(f32)
    for k in range(1, parts.shape[0]):
        total = total + parts[k].astype(f32)
    return total


def state_kernel(parts, offsets, gain, pieces, unit_out, mixed_out, rms_out):
    mixed = sum_pieces(parts)
    state = mixed + offsets[...]
    rms = jnp.sqrt(jnp.mean(state * state, axis=1, keepdims=True) + NORM_EPS)
    unit = state / rms
    unit_out[...] = unit
    mixed_out[...] = mixed
    rms_out[...] = jnp.broadcast_to(rms, rms_out.shape)
    value = (unit * gain[...]).astype(bf16)
    for k in range(pieces.shape[0]):
        pieces[k] = value


def state_call(parts, offsets, gain):
    piece, width = offsets.shape
    return call(
        state_kernel,
        [parts, offsets, gain],
        [
            jax.ShapeDtypeStruct(parts.shape, bf16),
            jax.ShapeDtypeStruct((piece, width), f32),
            jax.ShapeDtypeStruct((piece, width), f32),
            jax.ShapeDtypeStruct((piece, LANES), f32),
        ],
    )


def offset_kernel(parts, unit, mixed, rms, gain, pieces):
    sums = sum_pieces(parts)
    piece, width = unit.shape
    scaled = sums[:, :width] * gain[...]
    along = jnp.mean(scaled * unit[...], axis=1, keepdims=True)
    value = ((scaled - unit[...] * along) / rms[:, :1]).astype(bf16).astype(f32)
    inner = jnp.sum(value * mixed[...], axis=1, keepdims=True)
    share = sums[0:1, width:] + sums[1:2, width:] + sums[2:3, width:]
    share = jnp.concatenate(list(in_thirds(share)) + [jnp.zeros_like(share)], axis=0)
    lane = lax.broadcasted_iota(jnp.int32, (piece, LANES), 1)
    terms = jnp.zeros((piece, LANES), f32)
    for k, term in enumerate(in_thirds(inner)):
        terms = jnp.where(lane == k, term, terms)
    line = jnp.concatenate([value, share, terms], axis=1).astype(bf16)
    for k in range(pieces.shape[0]):
        pieces[k] = line


def offset_call(parts, unit, mixed, rms, gain):
    n, piece, _ = parts.shape
    return call(
        offset_kernel,
        [parts, unit, mixed, rms, gain],
        [jax.ShapeDtypeStruct((n, piece, unit.shape[1] + 2 * LANES), bf16)],
    )[0]


def first_grad_kernel(half, assemble, *refs):
    if assemble:
        first, pieces, logits, rows, targets, adv, table, grad, hidden, inner_out, gain = refs
        width = hidden.shape[1]
        gather_rows(pieces, hidden)
        terms = [pieces[k, :, width + LANES :].astype(f32) for k in range(pieces.shape[0])]
        terms = jnp.concatenate(terms, axis=0).T
        inner = terms[0:1, :] + terms[1:2, :] + terms[2:3, :]
        inner_out[...] = jnp.broadcast_to(inner, inner_out.shape)
        for k in range(gain.shape[0]):
            share = pieces[k, :, width : width + LANES].astype(f32)
            gain[k : k + 1, :] = share[0:1] + share[1:2] + share[2:3]
    else:
        first, hidden, logits, rows, targets, adv, table, inner_in, grad = refs
        inner = inner_in[0:1, :]
    block = table.shape[0]
    lse, mean = rows[0:1, :], rows[1:2, :]
    for start in range(0, block, VOCAB_TILE):
        prob_grad = nt(table[start : start + VOCAB_TILE, :], hidden[...])
        tile = logits[half * block + start : half * block + start + VOCAB_TILE, :]
        probs = jnp.exp(tile - lse)
        entries = entries_of(first[half] + start, *tile.shape)
        value = logit_grad(tile, probs, mean, adv[...], entries, targets[...])
        value = value + probs * (prob_grad - inner)
        grad[start : start + VOCAB_TILE, :] = value.astype(bf16)


def first_grad_call(hidden, logits, half, rows, targets, adv, table, first, inner=None):
    block, width = table.shape
    n_rows = logits.shape[1]
    out_shape = [jax.ShapeDtypeStruct((block, n_rows), bf16)]
    operands = [first, hidden, in_vmem(logits), rows, targets, adv, in_vmem(table)]
    if inner is None:
        out_shape += [
            jax.ShapeDtypeStruct((n_rows, width), bf16),
            jax.ShapeDtypeStruct((8, n_rows), f32),
            jax.ShapeDtypeStruct((width // LANES, LANES), f32),
        ]
    else:
        operands.append(inner)
    return call(
        functools.partial(first_grad_kernel, half, inner is None), operands, out_shape, (), 1
    )


def head_kernel(n, place, *refs):
    lefts, rights = refs[:n], refs[n : 2 * n]
    mine, theirs, gain_a, gain_b, head, offset, gain = refs[2 * n :]
    block = head.shape[0]
    half = offset.shape[0] // 2

    @pl.when(pl.program_id(0) == 0)
    def _():
        gain[...] = gain_a[...] + gain_b[...]
        at = pl.ds(pl.multiple_of(place[0] * half, half), half)
        low = place[1] == 0
        offset[:half, :] = jnp.where(low, mine[at, :], theirs[at, :])
        offset[half:, :] = jnp.where(low, theirs[at, :], mine[at, :])

    start = pl.multiple_of(pl.program_id(0) * WIDTH_TILE, WIDTH_TILE)
    left = jnp.concatenate([r[:block, :] for r in lefts], axis=1)
    right = jnp.concatenate([r[:, pl.ds(start, WIDTH_TILE)] for r in rights], axis=0)
    head[...] = jnp.dot(left, right, preferred_element_type=f32)


def head_call(pairs, block, place, offset_rows, offset_other, gain_a, gain_b, own_rows):
    width = pairs[0][1].shape[1]
    operands = [p[0] for p in pairs] + [p[1] for p in pairs]
    operands += [offset_rows, offset_other, gain_a, gain_b]
    return pl.pallas_call(
        functools.partial(head_kernel, len(pairs)),
        grid=(width // WIDTH_TILE,),
        in_specs=[pl.BlockSpec(memory_space=pltpu.SMEM)] + [whole()] * len(operands),
        out_shape=[
            jax.ShapeDtypeStruct((block, width), f32),
            jax.ShapeDtypeStruct((own_rows, width), bf16),
            jax.ShapeDtypeStruct(gain_a.shape, f32),
        ],
        out_specs=[pl.BlockSpec((block, WIDTH_TILE), lambda i: (0, i)), whole(), whole()],
        compiler_params=pltpu.CompilerParams(vmem_limit_bytes=24 * 1024 * 1024),
    )(place, *operands)


def local(start_hidden, offsets, norm_gain, head_table, targets_one, targets_two, advantage):
    core = lax.axis_index("c")
    sub = lax.axis_index(("x", "zl"))
    n_dp = lax.axis_size(DP)
    n_chip = lax.axis_size(CHIPS)
    own_rows, width = start_hidden.shape
    half = own_rows // 2
    rows = n_dp * half
    piece = rows // n_chip
    block_rows = head_table.shape[0]

    def core_rows(values):
        grouped = values.reshape(n_dp, 2, half)
        return lax.dynamic_slice_in_dim(grouped, core, 1, 1).reshape(1, rows)

    first = (lax.axis_index(DP) * lax.axis_size(VOCAB) + lax.axis_index(VOCAB)) * block_rows
    first = jnp.stack([first, first + (1 - 2 * core) * block_rows])
    tg_one = core_rows(targets_one)
    tg_two = core_rows(targets_two)
    adv = core_rows(advantage).astype(f32)
    gain = norm_gain[None, :]
    own_offsets = lax.dynamic_slice_in_dim(offsets, core * half + sub * piece, piece, 0).astype(f32)
    place = jnp.stack([lax.axis_index(DP), core])
    tables = (head_table, swap(head_table))

    own_half = lax.dynamic_slice_in_dim(start_hidden, core * half, half, 0)
    hidden = spread(own_half, DP).reshape(rows, width)
    hidden, first, tg_one, tg_two, adv, gain, own_offsets, place = together(
        hidden, first, tg_one, tg_two, adv, gain, own_offsets, place
    )
    hidden_other = swap(hidden)
    logits_one, stats, *tables = logits_call(hidden, tables, n_chip)
    stats, hidden_other = together(stats, hidden_other)
    low, partial, rows_one = mixture_call(logits_one, exchange(stats, CHIPS), tables)
    pieces, unit, mixed, rms = state_call(exchange(partial, CHIPS), own_offsets, gain)

    pieces, low = together(exchange(pieces, CHIPS), low)
    low_other = swap(low[block_rows:])
    logits_two, stats, next_input = logits_call(pieces, tables, n_chip)
    stats, low_other = together(stats, low_other)
    stats, next_input = together(exchange(stats, CHIPS), next_input)
    next_other = swap(next_input)
    grad_two, partial, _ = mixture_call(
        logits_two, stats, tables, (first, tg_two, adv, next_input, gain)
    )
    partial, next_other = together(partial, next_other)
    pieces = offset_call(exchange(partial, CHIPS), unit, mixed, rms, gain)
    pieces, grad_two = together(exchange(pieces, CHIPS), grad_two)
    two_other = swap(grad_two[block_rows:])

    grad_b, offset_rows, inner, gain_half = first_grad_call(
        pieces, logits_one, 1, rows_one, tg_one, adv, tables[1], first
    )
    one_other = swap(grad_b)
    offset_other = swap(offset_rows)
    (grad_a,) = first_grad_call(
        offset_rows, logits_one, 0, rows_one, tg_one, adv, tables[0], first, inner
    )
    head_grad, offset_grad, gain_grad = head_call(
        [
            (grad_two, next_input),
            (two_other, next_other),
            (low, offset_rows),
            (grad_a, hidden),
            (low_other, offset_other),
            (one_other, hidden_other),
        ],
        block_rows,
        place,
        offset_rows,
        offset_other,
        gain_half,
        swap(gain_half),
        own_rows,
    )
    return (head_grad, gain_grad.reshape(width), offset_grad)


def solution(mesh):
    fine = Mesh(mesh.devices.reshape(2, 4, 4, 2, 2), ("zh", "y", "x", "zl", "c"))
    rows = DP + VOCAB
    return jax.shard_map(
        local,
        mesh=fine,
        in_specs=(P(DP, None), P(DP, None), P(), P(rows, None), P(), P(), P()),
        out_specs=(P(rows, None), P(), P(DP, None)),
        check_vma=False,
    )
```

profile of v0, /device:TPU:1, one launch (start us, length us, event | category | flops | bytes accessed | tf_op | source)
XLA Modules:
  0.0 229.5 jit_solution(11689641527937308793)
XLA Ops:
  0.6 1.5 collective-permute-start
  2.2 1.3 broadcast_in_dim.4
  3.5 7.9 %all-to-all-start = ((bf16[8,32,3072]{2,1,0:T(8,128)(2,1)}), bf16[8,32,3072]{2,1,0:T(8,128)(2,1)S(1)}, u32[]{:S(2)}, u32[]{:S(2)}) async-start(bf16[8,32,3072]{2,1,0:T(8,128)(2,1)} %broadcast_in_dim.4), calls=%async_computation | async-start | bytes 3145728 | tf_op jit(solution)/shard_map/all_to_all | solution.py:28
  11.4 0.1 reshape.43
  11.5 0.1 reshape.45
  11.7 0.1 reshape.46.refs_3_
  11.8 0.1 reshape.47
  12.1 0.8 dynamic-slice_convert_fusion.offsets
  12.9 21.5 %all-to-all-done = bf16[8,32,3072]{2,1,0:T(8,128)(2,1)S(1)} async-done(((bf16[8,32,3072]{2,1,0:T(8,128)(2,1)}), bf16[8,32,3072]{2,1,0:T(8,128)(2,1)S(1)}, u32[]{:S(2)}, u32[]{:S(2)}) %all-to-all-start) | async-done | bytes 1572896 | tf_op jit(solution)/shard_map/all_to_all | solution.py:28
  34.4 0.8 collective-permute-start.1
  35.2 10.1 %shard_map.94 = (f32[2048,256]{1,0:T(8,128)S(1)}, f32[64,8,128]{2,1,0:T(8,128)S(1)}, bf16[1024,3072]{1,0:T(8,128)(2,1)S(1)}, bf16[1024,3072]{1,0:T(8,128)(2,1)S(1)}) custom-call(bf16[256,3072]{1,0:T(8,128)(2,1)S(1)} %bitcast.8, bf16[1024,3072]{1,0:T(8,128)(2,1)} %refs_1_.1, bf16[1024,3072]{1,0:T(8,128)(2,1)} %collective-permute-done.refs_2_), custom_call_target="tpu_custom_call" | custom-call | tf_op jit(solution)/shard_map/pallas_call | solution.py:49
  45.4 16.0 %all_to_all.35.refs_1_ = f32[64,8,128]{2,1,0:T(8,128)S(1)} all-to-all(f32[64,8,128]{2,1,0:T(8,128)S(1)} %get-tuple-element.51), channel_id=1, replica_groups=mesh['zh'=2,'y'=4,'x'=4,'zl'=2,'c'=2] {'zh','y','x','zl'}, dimensions={0} | all-to-all | bytes 524288 | tf_op jit(solution)/shard_map/all_to_all | solution.py:28
  61.4 3.6 %shard_map.95 = (bf16[2048,256]{1,0:T(8,128)(2,1)S(1)}, bf16[64,4,3072]{2,1,0:T(4,128)(2,1)S(1)}, f32[8,256]{1,0:T(8,128)S(1)}) custom-call(f32[2048,256]{1,0:T(8,128)S(1)} %get-tuple-element.49.refs_0_.refs_2_, f32[64,8,128]{2,1,0:T(8,128)S(1)} %all_to_all.35.refs_1_, bf16[1024,3072]{1,0:T(8,128)(2,1)S(1)} %get-tuple-element.52.refs_2_.refs_1_.refs_5_.refs_6_, ...), custom_call_target="tpu_custom_call" | custom-call | tf_op jit(solution)/shard_map/pallas_call | solution.py:49
  65.0 26.1 %all_to_all.36.parts = bf16[64,4,3072]{2,1,0:T(4,128)(2,1)S(1)} all-to-all(bf16[64,4,3072]{2,1,0:T(4,128)(2,1)S(1)} %get-tuple-element.54), channel_id=1, replica_groups=mesh['zh'=2,'y'=4,'x'=4,'zl'=2,'c'=2] {'zh','y','x','zl'}, dimensions={0} | all-to-all | bytes 3145728 | tf_op jit(solution)/shard_map/all_to_all | solution.py:28
  91.1 0.4 shard_map.96
  91.5 28.0 %all_to_all.37.refs_0_ = bf16[64,4,3072]{2,1,0:T(4,128)(2,1)S(1)} all-to-all(bf16[64,4,3072]{2,1,0:T(4,128)(2,1)S(1)} %get-tuple-element.57), channel_id=1, replica_groups=mesh['zh'=2,'y'=4,'x'=4,'zl'=2,'c'=2] {'zh','y','x','zl'}, dimensions={0} | all-to-all | bytes 3145728 | tf_op jit(solution)/shard_map/all_to_all | solution.py:28
  119.6 2.9 %collective-permute-start.2 = (bf16[1024,256]{1,0:T(8,128)(2,1)S(1)}, bf16[1024,256]{1,0:T(8,128)(2,1)S(1)}, u32[]{:S(2)}, u32[]{:S(2)}) collective-permute-start(bf16[1024,256]{1,0:T(8,128)(2,1)S(1)} %slice.6), channel_id=1, source_target_pairs={{0,1},{1,0},{2,3},{3,2},{4,5},{5,4},{6,7},{7,6},{8,9},{9,8},{10,11... | collective-permute-start | bytes 1572872 | tf_op jit(solution)/shard_map/ppermute | solution.py:24
  122.5 4.0 %shard_map.97 = (f32[2048,256]{1,0:T(8,128)S(1)}, f32[64,8,128]{2,1,0:T(8,128)S(1)}, bf16[256,3072]{1,0:T(8,128)(2,1)S(1)}) custom-call(bf16[64,4,3072]{2,1,0:T(4,128)(2,1)S(1)} %all_to_all.37.refs_0_, bf16[1024,3072]{1,0:T(8,128)(2,1)S(1)} %get-tuple-element.52.refs_2_.refs_1_.refs_5_.refs_6_, bf16[1024,3072]{1,0:T(8,128)(2,1)S(1)} %get-tuple-element.53.refs_3_.refs_2_.refs_6_), custom_call_target="tpu_custom_call" | custom-call | tf_op jit(solution)/shard_map/pallas_call | solution.py:49
  126.6 15.6 %all_to_all.38.refs_2_ = f32[64,8,128]{2,1,0:T(8,128)S(1)} all-to-all(f32[64,8,128]{2,1,0:T(8,128)S(1)} %get-tuple-element.63), channel_id=1, replica_groups=mesh['zh'=2,'y'=4,'x'=4,'zl'=2,'c'=2] {'zh','y','x','zl'}, dimensions={0} | all-to-all | bytes 524288 | tf_op jit(solution)/shard_map/all_to_all | solution.py:28
  142.2 1.4 collective-permute-start.3
  143.5 5.3 %shard_map.98 = (bf16[2048,256]{1,0:T(8,128)(2,1)S(1)}, bf16[64,4,3200]{2,1,0:T(4,128)(2,1)S(1)}, f32[8,256]{1,0:T(8,128)}) custom-call(s32[2]{0:T(128)S(1)} %get-tuple-element.47.refs_0_, f32[2048,256]{1,0:T(8,128)S(1)} %get-tuple-element.60.refs_1_, f32[64,8,128]{2,1,0:T(8,128)S(1)} %all_to_all.38.refs_2_, s32[1,256]{1,0:T(1,128)S(1)} %reshape.46.refs_3_, ...), custom_call_target="tpu_custom_call" | custom-call | tf_op jit(solution)/shard_map/pallas_call | solution.py:49
  148.8 28.4 %all_to_all.39.parts = bf16[64,4,3200]{2,1,0:T(4,128)(2,1)S(1)} all-to-all(bf16[64,4,3200]{2,1,0:T(4,128)(2,1)S(1)} %get-tuple-element.70), channel_id=1, replica_groups=mesh['zh'=2,'y'=4,'x'=4,'zl'=2,'c'=2] {'zh','y','x','zl'}, dimensions={0} | all-to-all | bytes 3276800 | tf_op jit(solution)/shard_map/all_to_all | solution.py:28
  177.2 0.5 shard_map.99
  177.7 28.8 %all_to_all.40.refs_1_ = bf16[64,4,3328]{2,1,0:T(4,128)(2,1)S(1)} all-to-all(bf16[64,4,3328]{2,1,0:T(4,128)(2,1)S(1)} %shard_map.99), channel_id=1, replica_groups=mesh['zh'=2,'y'=4,'x'=4,'zl'=2,'c'=2] {'zh','y','x','zl'}, dimensions={0} | all-to-all | bytes 3407872 | tf_op jit(solution)/shard_map/all_to_all | solution.py:28
  206.5 2.7 %shard_map.100 = (bf16[1024,256]{1,0:T(8,128)(2,1)S(1)}, bf16[256,3072]{1,0:T(8,128)(2,1)S(1)}, f32[8,256]{1,0:T(8,128)S(1)}, f32[24,128]{1,0:T(8,128)S(1)}) custom-call(s32[2]{0:T(128)S(1)} %get-tuple-element.47.refs_0_, bf16[64,4,3328]{2,1,0:T(4,128)(2,1)S(1)} %all_to_all.40.refs_1_, f32[2048,256]{1,0:T(8,128)S(1)} %get-tuple-element.49.refs_0_.refs_2_, ...), custom_call_target="tpu_custom_call" | custom-call | tf_op jit(solution)/shard_map/pallas_call | solution.py:49
  209.2 2.9 %collective-permute-start.6 = (bf16[256,3072]{1,0:T(8,128)(2,1)S(1)}, bf16[256,3072]{1,0:T(8,128)(2,1)S(1)}, u32[]{:S(2)}, u32[]{:S(2)}) collective-permute-start(bf16[256,3072]{1,0:T(8,128)(2,1)S(1)} %get-tuple-element.79.refs_1_.refs_8_.refs_12_), channel_id=1, source_target_pairs={{0,1},{1,0},{2,3},{3,2},{4,5},{5,4},{6,7},{7,6},{8,9},{9,8},{10,11... | collective-permute-start | bytes 4718600 | tf_op jit(solution)/shard_map/ppermute | solution.py:24
  212.1 0.1 collective-permute-start.4
  212.2 0.5 collective-permute-start.5
  212.7 0.1 collective-permute-start.7
  212.8 2.7 %shard_map.101.refs_3_ = bf16[1024,256]{1,0:T(8,128)(2,1)S(1)} custom-call(s32[2]{0:T(128)S(1)} %get-tuple-element.47.refs_0_, bf16[256,3072]{1,0:T(8,128)(2,1)S(1)} %get-tuple-element.79.refs_1_.refs_8_.refs_12_, f32[2048,256]{1,0:T(8,128)S(1)} %get-tuple-element.49.refs_0_.refs_2_, f32[8,256]{1,0:T(8,128)S(1)} %get-tuple-element.77.refs_3_, ...), custom_call_target="tpu_custom_call" | custom-call | tf_op jit(solution)/shard_map/pallas_call | solution.py:49
  215.5 1.1 collective-permute-done.7.refs_15_
  216.6 12.9 %shard_map.102 = (f32[1024,3072]{1,0:T(8,128)}, bf16[64,3072]{1,0:T(8,128)(2,1)}, f32[24,128]{1,0:T(8,128)}) custom-call(s32[2]{0:T(128)S(1)} %get-tuple-element.46.place, bf16[2048,256]{1,0:T(8,128)(2,1)S(1)} %get-tuple-element.75.refs_0_, bf16[1024,256]{1,0:T(8,128)(2,1)S(1)} %collective-permute-done.4.refs_1_, ...), custom_call_target="tpu_custom_call" | custom-call | tf_op jit(solution)/shard_map/pallas_call | solution.py:369
  (27 shorter events, 0.4 us)
Async XLA Ops:
  0.6 1.5 copy-start
  0.6 34.6 %collective-permute-start = (bf16[1024,3072]{1,0:T(8,128)(2,1)}, bf16[1024,3072]{1,0:T(8,128)(2,1)}, u32[]{:S(2)}, u32[]{:S(2)}) collective-permute-start(bf16[1024,3072]{1,0:T(8,128)(2,1)} %refs_1_.1), channel_id=1, source_target_pairs={{0,1},{1,0},{2,3},{3,2},{4,5},{5,4},{6,7},{7,6},{8,9},{9,8},{10,11... | collective-permute-start | bytes 18874376 | tf_op jit(solution)/shard_map/ppermute | solution.py:24
  3.5 8.0 %copy-start.3 = (s32[512]{0:T(512)S(1)}, s32[512]{0:T(512)}, u32[]{:S(2)}) copy-start(s32[512]{0:T(512)} %param.11) | copy-start | bytes 6148
  3.5 8.0 %copy-start.4 = (s32[512]{0:T(512)S(1)}, s32[512]{0:T(512)}, u32[]{:S(2)}) copy-start(s32[512]{0:T(512)} %param.12) | copy-start | bytes 6148
  3.5 8.3 %copy-start.5 = (s32[512]{0:T(512)S(1)}, s32[512]{0:T(512)}, u32[]{:S(2)}) copy-start(s32[512]{0:T(512)} %param.13) | copy-start | bytes 6148
  3.5 30.9 %all-to-all-start = ((bf16[8,32,3072]{2,1,0:T(8,128)(2,1)}), bf16[8,32,3072]{2,1,0:T(8,128)(2,1)S(1)}, u32[]{:S(2)}, u32[]{:S(2)}) async-start(bf16[8,32,3072]{2,1,0:T(8,128)(2,1)} %broadcast_in_dim.4), calls=%async_computation | async-start | bytes 3145728 | tf_op jit(solution)/shard_map/all_to_all | solution.py:28
  34.4 11.0 %collective-permute-start.1 = (bf16[256,3072]{1,0:T(8,128)(2,1)S(1)}, bf16[256,3072]{1,0:T(8,128)(2,1)S(1)}, u32[]{:S(2)}, u32[]{:S(2)}) collective-permute-start(bf16[256,3072]{1,0:T(8,128)(2,1)S(1)} %bitcast.7), channel_id=1, source_target_pairs={{0,1},{1,0},{2,3},{3,2},{4,5},{5,4},{6,7},{7,6},{8,9},{9,8},{10,11... | collective-permute-start | bytes 4718600 | tf_op jit(solution)/shard_map/ppermute | solution.py:24
  65.0 26.1 %copy-start.2 = (f32[3072]{0:T(1024)S(1)}, f32[3072]{0:T(1024)}, u32[]{:S(2)}) copy-start(f32[3072]{0:T(1024)} %param.9) | copy-start | bytes 36868
  119.6 6.9 %collective-permute-start.2 = (bf16[1024,256]{1,0:T(8,128)(2,1)S(1)}, bf16[1024,256]{1,0:T(8,128)(2,1)S(1)}, u32[]{:S(2)}, u32[]{:S(2)}) collective-permute-start(bf16[1024,256]{1,0:T(8,128)(2,1)S(1)} %slice.6), channel_id=1, source_target_pairs={{0,1},{1,0},{2,3},{3,2},{4,5},{5,4},{6,7},{7,6},{8,9},{9,8},{10,11... | collective-permute-start | bytes 1572872 | tf_op jit(solution)/shard_map/ppermute | solution.py:24
  142.2 6.6 %collective-permute-start.3 = (bf16[256,3072]{1,0:T(8,128)(2,1)S(1)}, bf16[256,3072]{1,0:T(8,128)(2,1)S(1)}, u32[]{:S(2)}, u32[]{:S(2)}) collective-permute-start(bf16[256,3072]{1,0:T(8,128)(2,1)S(1)} %get-tuple-element.68.refs_7_.refs_6_), channel_id=1, source_target_pairs={{0,1},{1,0},{2,3},{3,2},{4,5},{5,4},{6,7},{7,6},{8,9},{9,8},{10,11... | collective-permute-start | bytes 4718600 | tf_op jit(solution)/shard_map/ppermute | solution.py:24
  209.2 7.4 %collective-permute-start.6 = (bf16[256,3072]{1,0:T(8,128)(2,1)S(1)}, bf16[256,3072]{1,0:T(8,128)(2,1)S(1)}, u32[]{:S(2)}, u32[]{:S(2)}) collective-permute-start(bf16[256,3072]{1,0:T(8,128)(2,1)S(1)} %get-tuple-element.79.refs_1_.refs_8_.refs_12_), channel_id=1, source_target_pairs={{0,1},{1,0},{2,3},{3,2},{4,5},{5,4},{6,7},{7,6},{8,9},{9,8},{10,11... | collective-permute-start | bytes 4718600 | tf_op jit(solution)/shard_map/ppermute | solution.py:24
  212.1 4.5 %collective-permute-start.4 = (bf16[1024,256]{1,0:T(8,128)(2,1)S(1)}, bf16[1024,256]{1,0:T(8,128)(2,1)S(1)}, u32[]{:S(2)}, u32[]{:S(2)}) collective-permute-start(bf16[1024,256]{1,0:T(8,128)(2,1)S(1)} %slice.7), channel_id=1, source_target_pairs={{0,1},{1,0},{2,3},{3,2},{4,5},{5,4},{6,7},{7,6},{8,9},{9,8},{10,11... | collective-permute-start | bytes 1572872 | tf_op jit(solution)/shard_map/ppermute | solution.py:24
  212.2 4.4 %collective-permute-start.5 = (bf16[1024,256]{1,0:T(8,128)(2,1)S(1)}, bf16[1024,256]{1,0:T(8,128)(2,1)S(1)}, u32[]{:S(2)}, u32[]{:S(2)}) collective-permute-start(bf16[1024,256]{1,0:T(8,128)(2,1)S(1)} %get-tuple-element.82), channel_id=1, source_target_pairs={{0,1},{1,0},{2,3},{3,2},{4,5},{5,4},{6,7},{7,6},{8,9},{9,8},{10,11... | collective-permute-start | bytes 1572872 | tf_op jit(solution)/shard_map/ppermute | solution.py:24
  212.7 3.9 %collective-permute-start.7 = (f32[24,128]{1,0:T(8,128)S(1)}, f32[24,128]{1,0:T(8,128)S(1)}, u32[]{:S(2)}, u32[]{:S(2)}) collective-permute-start(f32[24,128]{1,0:T(8,128)S(1)} %get-tuple-element.85.refs_14_), channel_id=1, source_target_pairs={{0,1},{1,0},{2,3},{3,2},{4,5},{5,4},{6,7},{7,6},{8,9},{9,8},{10,11... | collective-permute-start | bytes 36872 | tf_op jit(solution)/shard_map/ppermute | solution.py:24
  216.6 12.9 %copy-start.1 = (bf16[64,3072]{1,0:T(8,128)(2,1)S(1)}, bf16[64,3072]{1,0:T(8,128)(2,1)}, u32[]{:S(2)}) copy-start(bf16[64,3072]{1,0:T(8,128)(2,1)} %param.7) | copy-start | bytes 1179652
where the time goes:
time: 230 us
  blocking collectives  143 us (62%)
  Pallas kernels  42.3 us (18%)
  waiting for transfers between devices  22.6 us (10%)
  starting transfers between devices  18.1 us (8%)
    all_to_all x6, blocking collectives, exchange(): return lax.all_to_all(blocks, axes, 0, 0)  143 us
    pallas_call x8, Pallas kernels, call(): pl.pallas_call(kernel, in_specs=specs, out_shape=out_shape, out_specs=[wh...  29.4 us
    all_to_all x1, waiting for transfers between devices, exchange(): return lax.all_to_all(blocks, axes, 0, 0)  21.5 us
    pallas_call x1, Pallas kernels, head_call(): pl.pallas_call(functools.partial(head_kernel, len(pairs)), grid=(width //...  12.9 us
    ppermute x8, starting transfers between devices, swap(): return lax.ppermute(value, 'c', SWAP)  10.2 us
    all_to_all x1, starting transfers between devices, exchange(): return lax.all_to_all(blocks, axes, 0, 0)  7.95 us
  transfers between devices with their start and end apart: 9, of which 2 were waited for; matrix products, arithmetic and copies ran while one was open for 1% of the time, Pallas kernels for 10%

commit v1 on v0

v1 whole, which is shorter than its diff:
```python
import functools

import jax
import jax.numpy as jnp
from jax import lax
from jax.experimental import pallas as pl
from jax.experimental.pallas import tpu as pltpu
from jax.sharding import Mesh, PartitionSpec as P

ENTROPY_WEIGHT = 0.05
NORM_EPS = 1e-05
DP = ("zh", "y")
VOCAB = ("x", "zl", "c")
CHIPS = ("zh", "y", "x", "zl")
SWAP = [(0, 1), (1, 0)]
VOCAB_TILE = 256
WIDTH_TILE = 512
HEAD_TILE = 256
LANES = 128
f32 = jnp.float32
bf16 = jnp.bfloat16


def swap(value):
    return lax.ppermute(value, "c", SWAP)


def exchange(blocks, axes):
    return lax.all_to_all(blocks, axes, 0, 0)


def whole():
    return pl.BlockSpec(memory_space=pltpu.VMEM)


def in_vmem(value):
    return pltpu.with_memory_space_constraint(value, pltpu.VMEM)


def call(kernel, operands, out_shape, scratch_shapes=(), scalars=0, vmem=16, far=()):
    specs = [pl.BlockSpec(memory_space=pltpu.SMEM)] * scalars
    specs += [whole()] * (len(operands) - scalars)
    for k in far:
        specs[k] = pl.BlockSpec(memory_space=pl.ANY)
    return pl.pallas_call(
        kernel,
        in_specs=specs,
        out_shape=out_shape,
        out_specs=[whole()] * len(out_shape),
        scratch_shapes=scratch_shapes,
        compiler_params=pltpu.CompilerParams(vmem_limit_bytes=vmem * 1024 * 1024),
    )(*operands)


def gather_rows(pieces_ref, rows_ref):
    width = rows_ref.shape[1]
    for j in range(rows_ref.shape[0] // 16):
        part = [pieces_ref[4 * j + k, :, :width].astype(f32) for k in range(4)]
        rows_ref[16 * j : 16 * j + 16, :] = jnp.concatenate(part, axis=0).astype(bf16)


def scatter_rows(value, pieces_ref, start):
    for j in range(value.shape[0] // 4):
        pieces_ref[j, :, start : start + value.shape[1]] = value[4 * j : 4 * j + 4].astype(bf16)


def nt(left, right):
    return lax.dot_general(left, right, (((1,), (1,)), ((), ())), preferred_element_type=f32)


def together(*values):
    return lax.optimization_barrier(values)


def in_lines(row):
    return [row[:, k : k + LANES] for k in range(0, row.shape[1], LANES)]


def start_kernel(place, hidden, offsets, *refs):
    given, table = refs[:3], refs[3]
    spread_out, own_offsets, aux, own, offset_rows, lines, sems = refs[4:]
    low = place[3] == 0
    n_dp, half, _ = spread_out.shape
    mine = hidden.at[pl.ds(pl.multiple_of(place[3] * half, half), half)]
    moves = [(mine, spread_out.at[k]) for k in range(n_dp)]
    moves += [(offsets, offset_rows)] + [(v, lines.at[k]) for k, v in enumerate(given)]
    moves += [(table, own)]
    copies = [pltpu.make_async_copy(f, t, sems.at[k]) for k, (f, t) in enumerate(moves)]
    for copy in copies:
        copy.start()
    for copy in copies[n_dp:-1]:
        copy.wait()
    piece = own_offsets.shape[0]
    values = offset_rows[...].astype(f32)
    chosen = values[:piece]
    for k in range(1, values.shape[0] // piece):
        chosen = jnp.where(place[4] == k, values[piece * k : piece * (k + 1)], chosen)
    own_offsets[...] = chosen
    rows = []
    for k in range(len(given)):
        values = lines[k]
        parts = []
        for d in range(n_dp):
            line, lane = divmod(2 * half * d, LANES)
            first = values[line : line + 1, lane : lane + half]
            second = values[line : line + 1, lane + half : lane + 2 * half]
            parts.append(jnp.where(low, first, second))
        rows.append(jnp.concatenate(parts, axis=1))
    aux[...] = jnp.concatenate(rows + [rows[0]] * 5, axis=0)
    for copy in copies[:n_dp] + copies[-1:]:
        copy.wait()


def start_call(place, start_hidden, offsets, targets_one, targets_two, advantage, table, n_dp, piece):
    own_rows, width = start_hidden.shape
    half = own_rows // 2
    lines = [v.reshape(-1, LANES) for v in (targets_one, targets_two, advantage)]
    operands = [start_hidden, offsets, *lines, table]
    return call(
        start_kernel,
        [place] + [pltpu.with_memory_space_constraint(v, pltpu.HBM) for v in operands],
        [
            jax.ShapeDtypeStruct((n_dp, half, width), bf16),
            jax.ShapeDtypeStruct((piece, width), f32),
            jax.ShapeDtypeStruct((8, n_dp * half), jnp.int32),
            pltpu.VMEM(table.shape, bf16),
        ],
        [
            pltpu.VMEM((own_rows, width), bf16),
            pltpu.VMEM((3, *lines[0].shape), jnp.int32),
            pltpu.SemaphoreType.DMA((n_dp + 5,)),
        ],
        scalars=1,
        far=range(1, 7),
    )


def logits_kernel(second, *refs):
    if second:
        pieces, own, other, lse, before, logits, stats, hidden = refs
        gather_rows(pieces, hidden)
    else:
        hidden, own, other, logits, stats, local_out = refs
    n_rows = logits.shape[1]
    block = other.shape[0]
    old = jnp.full((1, n_rows), -1e30, f32)
    total = jnp.zeros((1, n_rows), f32)
    weighted = total
    for table, base in ((own, 0), (other, block)):
        for start in range(0, block, VOCAB_TILE):
            tile = nt(table[start : start + VOCAB_TILE, :], hidden[...])
            logits[base + start : base + start + VOCAB_TILE, :] = tile
            top = jnp.maximum(old, jnp.max(tile, axis=0, keepdims=True))
            shifted = tile - top
            expo = jnp.exp(shifted)
            scale = jnp.exp(old - top)
            weighted = scale * (weighted + (old - top) * total) + jnp.sum(
                expo * shifted, axis=0, keepdims=True
            )
            total = scale * total + jnp.sum(expo, axis=0, keepdims=True)
            old = top
    log_total = old + jnp.log(total)
    mean = old + weighted / total
    lines = in_lines(log_total)
    if second:
        lines += in_lines(mean)
        lines += in_lines(jnp.exp(before[0:1, :] - lse[0:1, :]) * before[1:2, :])
    else:
        local_out[...] = jnp.concatenate([log_total, mean] + [mean] * 6, axis=0)
    lines += [jnp.zeros((1, LANES), f32)] * (stats.shape[1] - len(lines))
    stats[...] = jnp.broadcast_to(jnp.concatenate(lines, axis=0)[None], stats.shape)


def first_logits_call(hidden, table, other, n_chip):
    block, width = table.shape
    rows = hidden.shape[0]
    return call(
        functools.partial(logits_kernel, False),
        [hidden, in_vmem(table), in_vmem(other)],
        [
            pltpu.VMEM((2 * block, rows), f32),
            jax.ShapeDtypeStruct((n_chip, rows // LANES, LANES), f32),
            jax.ShapeDtypeStruct((8, rows), f32),
        ],
    )


def second_logits_call(pieces, tables, lse, before):
    block, width = tables[0].shape
    n_chip, piece, _ = pieces.shape
    rows = n_chip * piece
    return call(
        functools.partial(logits_kernel, True),
        [pieces, in_vmem(tables[0]), in_vmem(tables[1]), lse, before],
        [
            pltpu.VMEM((2 * block, rows), f32),
            jax.ShapeDtypeStruct((n_chip, 8, LANES), f32),
            jax.ShapeDtypeStruct((rows, width), bf16),
        ],
    )


def stat(stats, k, n_rows):
    n = n_rows // LANES
    return jnp.concatenate([stats[:, k * n + j, :] for j in range(n)], axis=1)


def all_lse(local_lse):
    peak = jnp.max(local_lse, axis=0, keepdims=True)
    return peak + jnp.log(jnp.sum(jnp.exp(local_lse - peak), axis=0, keepdims=True))


def logit_grad(logits, probs, mean, adv, entries, targets):
    onehot = (entries == targets).astype(f32)
    return -adv * (onehot - probs) + ENTROPY_WEIGHT * probs * (logits - mean)


def entries_of(first, n, rows):
    return first + lax.broadcasted_iota(jnp.int32, (n, rows), 0)


def mixture_kernel(with_grad, *refs):
    if with_grad:
        place, logits, stats, aux, own, other = refs[:6]
    else:
        logits, stats, own, other = refs[:4]
    coef, partial, rows, turned = refs[-4:]
    block, width = own.shape
    n_rows = logits.shape[1]
    local_lse = stat(stats, 0, n_rows)
    lse = all_lse(local_lse)
    row = lse
    if with_grad:
        adv = aux[2:3, :].astype(f32)
        weight = jnp.exp(local_lse - lse)
        mean = jnp.sum(weight * stat(stats, 1, n_rows), axis=0, keepdims=True)
        row = jnp.sum(stat(stats, 2, n_rows), axis=0, keepdims=True)
    rows[...] = jnp.broadcast_to(row, rows.shape)
    for start in range(0, 2 * block, VOCAB_TILE):
        tile = logits[start : start + VOCAB_TILE, :]
        probs = jnp.exp(tile - lse)
        if with_grad:
            entries = entries_of(place[start // block] + start % block, VOCAB_TILE, n_rows)
            probs = logit_grad(tile, probs, mean, adv, entries, aux[1:2, :])
        coef[start : start + VOCAB_TILE, :] = probs.astype(bf16)
        turned[:, start : start + VOCAB_TILE] = probs.T.astype(bf16)
    for start in range(0, width, WIDTH_TILE):
        columns = slice(start, start + WIDTH_TILE)
        value = jnp.dot(turned[:, :block], own[:, columns], preferred_element_type=f32)
        value = value + jnp.dot(turned[:, block:], other[:, columns], preferred_element_type=f32)
        scatter_rows(value, partial, start)


def mixture_call(logits, stats, tables, grad=None):
    block, width = tables[0].shape
    n_rows = logits.shape[1]
    tables = [in_vmem(t) for t in tables]
    operands = [in_vmem(logits), stats, *tables]
    if grad is not None:
        place, aux = grad
        operands = [place, in_vmem(logits), stats, aux, *tables]
    return call(
        functools.partial(mixture_kernel, grad is not None),
        operands,
        [
            jax.ShapeDtypeStruct((2 * block, n_rows), bf16),
            jax.ShapeDtypeStruct((n_rows // 4, 4, width), bf16),
            jax.ShapeDtypeStruct((8, n_rows), f32),
        ],
        [pltpu.VMEM((n_rows, 2 * block), bf16)],
        0 if grad is None else 1,
    )


def in_thirds(value):
    high = value.astype(bf16).astype(f32)
    middle = (value - high).astype(bf16).astype(f32)
    return high, middle, value - high - middle


def sum_pieces(parts):
    total = parts[0].astype(f32)
    for k in range(1, parts.shape[0]):
        total = total + parts[k].astype(f32)
    return total


def state_kernel(parts, offsets, gain, pieces, unit_out, mixed_out, rms_out):
    mixed = sum_pieces(parts)
    state = mixed + offsets[...]
    rms = jnp.sqrt(jnp.mean(state * state, axis=1, keepdims=True) + NORM_EPS)
    unit = state / rms
    unit_out[...] = unit
    mixed_out[...] = mixed
    rms_out[...] = jnp.broadcast_to(rms, rms_out.shape)
    value = (unit * gain[...]).astype(bf16)
    for k in range(pieces.shape[0]):
        pieces[k] = value


def state_call(parts, offsets, gain):
    piece, width = offsets.shape
    return call(
        state_kernel,
        [parts, offsets, gain],
        [
            jax.ShapeDtypeStruct(parts.shape, bf16),
            jax.ShapeDtypeStruct((piece, width), f32),
            jax.ShapeDtypeStruct((piece, width), f32),
            jax.ShapeDtypeStruct((piece, LANES), f32),
        ],
    )


def offset_kernel(parts, unit, mixed, rms, gain, pieces):
    piece, width = unit.shape
    scaled = sum_pieces(parts) * gain[...]
    along = jnp.mean(scaled * unit[...], axis=1, keepdims=True)
    value = ((scaled - unit[...] * along) / rms[:, :1]).astype(bf16).astype(f32)
    inner = jnp.sum(value * mixed[...], axis=1, keepdims=True)
    lane = lax.broadcasted_iota(jnp.int32, (piece, LANES), 1)
    terms = jnp.zeros((piece, LANES), f32)
    for k, term in enumerate(in_thirds(inner) + in_thirds(along) + in_thirds(rms[:, :1])):
        terms = jnp.where(lane == k, term, terms)
    line = jnp.concatenate([value, terms], axis=1).astype(bf16)
    for k in range(pieces.shape[0]):
        pieces[k] = line


def offset_call(parts, unit, mixed, rms, gain):
    n, piece, width = parts.shape
    return call(
        offset_kernel,
        [parts, unit, mixed, rms, gain],
        [jax.ShapeDtypeStruct((n, piece, width + LANES), bf16)],
    )[0]


def first_grad_kernel(half, assemble, *refs):
    if assemble:
        place, pieces, logits, lse, mean, aux, table, next_input, gain = refs[:9]
        grad, hidden, inner_out, share = refs[9:]
        n_rows, width = hidden.shape
        gather_rows(pieces, hidden)
        terms = [pieces[k, :, width:].astype(f32) for k in range(pieces.shape[0])]
        terms = jnp.concatenate(terms, axis=0)
        inner = terms.T
        inner = inner[0:1, :] + inner[1:2, :] + inner[2:3, :]
        inner_out[...] = jnp.broadcast_to(inner, inner_out.shape)
        along = terms[:, 3:4] + terms[:, 4:5] + terms[:, 5:6]
        rms = terms[:, 6:7] + terms[:, 7:8] + terms[:, 8:9]
        for start in range(0, width, WIDTH_TILE):
            columns = slice(start, start + WIDTH_TILE)
            given = next_input[:, columns].astype(f32)
            inverse = 1.0 / gain[:, columns]
            value = hidden[:, columns].astype(f32) * rms + given * inverse * along
            value = jnp.sum(value * given, axis=0, keepdims=True)
            share[:, columns] = value * inverse * inverse
    else:
        place, hidden, logits, lse, mean, aux, table, inner_in, grad = refs
        inner = inner_in[0:1, :]
    block = table.shape[0]
    adv = aux[2:3, :].astype(f32)
    for start in range(0, block, VOCAB_TILE):
        prob_grad = nt(table[start : start + VOCAB_TILE, :], hidden[...])
        tile = logits[half * block + start : half * block + start + VOCAB_TILE, :]
        probs = jnp.exp(tile - lse[0:1, :])
        entries = entries_of(place[half] + start, *tile.shape)
        value = logit_grad(tile, probs, mean[0:1, :], adv, entries, aux[0:1, :])
        value = value + probs * (prob_grad - inner)
        grad[start : start + VOCAB_TILE, :] = value.astype(bf16)


def first_grad_call(place, hidden, logits, half, lse, mean, aux, table, more):
    block, width = table.shape
    n_rows = logits.shape[1]
    out_shape = [jax.ShapeDtypeStruct((block, n_rows), bf16)]
    operands = [place, hidden, in_vmem(logits), lse, mean, aux, in_vmem(table), *more]
    assemble = hidden.ndim == 3
    if assemble:
        out_shape += [
            jax.ShapeDtypeStruct((n_rows, width), bf16),
            jax.ShapeDtypeStruct((8, n_rows), f32),
            jax.ShapeDtypeStruct((1, width), f32),
        ]
    return call(
        functools.partial(first_grad_kernel, half, assemble), operands, out_shape, (), 1
    )


def head_kernel(n, place, *refs):
    lefts, rights = refs[:n], refs[n : 2 * n]
    mine, theirs, gain_a, gain_b, head, offset, gain = refs[2 * n :]

    @pl.when(pl.program_id(0) == 0)
    def _():
        gain[...] = gain_a[...] + gain_b[...]
        half = offset.shape[0] // 2
        at = pl.ds(pl.multiple_of(place[2] * half, half), half)
        low = place[3] == 0
        offset[:half, :] = jnp.where(low, mine[at, :], theirs[at, :])
        offset[half:, :] = jnp.where(low, theirs[at, :], mine[at, :])

    tile, width = head.shape
    row = pl.ds(pl.multiple_of(pl.program_id(0) * tile, tile), tile)
    left = jnp.concatenate([r[row, :] for r in lefts], axis=1)
    for start in range(0, width, WIDTH_TILE):
        columns = slice(start, start + WIDTH_TILE)
        right = jnp.concatenate([r[:, columns] for r in rights], axis=0)
        head[:, columns] = jnp.dot(left, right, preferred_element_type=f32)


def head_call(pairs, block, place, offset_rows, offset_other, gain_a, gain_b, own_rows):
    width = pairs[0][1].shape[1]
    operands = [p[0] for p in pairs] + [p[1] for p in pairs]
    operands += [offset_rows, offset_other, gain_a, gain_b]
    return pl.pallas_call(
        functools.partial(head_kernel, len(pairs)),
        grid=(block // HEAD_TILE,),
        in_specs=[pl.BlockSpec(memory_space=pltpu.SMEM)] + [whole()] * len(operands),
        out_shape=[
            jax.ShapeDtypeStruct((block, width), f32),
            jax.ShapeDtypeStruct((own_rows, width), bf16),
            jax.ShapeDtypeStruct(gain_a.shape, f32),
        ],
        out_specs=[pl.BlockSpec((HEAD_TILE, width), lambda i: (i, 0)), whole(), whole()],
        compiler_params=pltpu.CompilerParams(vmem_limit_bytes=24 * 1024 * 1024),
    )(place, *operands)


def local(start_hidden, offsets, norm_gain, head_table, targets_one, targets_two, advantage):
    core = lax.axis_index("c")
    sub = lax.axis_index(("x", "zl"))
    n_dp = lax.axis_size(DP)
    n_chip = lax.axis_size(CHIPS)
    own_rows, width = start_hidden.shape
    half = own_rows // 2
    rows = n_dp * half
    piece = rows // n_chip
    block_rows = head_table.shape[0]

    first = (lax.axis_index(DP) * lax.axis_size(VOCAB) + lax.axis_index(VOCAB)) * block_rows
    other_first = first + (1 - 2 * core) * block_rows
    place = jnp.stack([first, other_first, lax.axis_index(DP), core, core * (half // piece) + sub])
    gain = norm_gain[None, :]

    own_half, own_offsets, aux, own = start_call(
        place, start_hidden, offsets, targets_one, targets_two, advantage, head_table, n_dp, piece
    )
    other = swap(own)
    hidden = exchange(own_half, DP).reshape(rows, width)
    hidden_other = swap(hidden)
    logits_one, stats, before = first_logits_call(hidden, own, other, n_chip)
    tables = (own, other)
    stats, hidden_other = together(stats, hidden_other)
    low, partial, lse_one = mixture_call(logits_one, exchange(stats, CHIPS), tables)
    pieces, unit, mixed, rms = state_call(exchange(partial, CHIPS), own_offsets, gain)

    pieces, low = together(exchange(pieces, CHIPS), low)
    low_other = swap(low[block_rows:])
    logits_two, stats, next_input = second_logits_call(pieces, tables, lse_one, before)
    stats, low_other = together(stats, low_other)
    stats, next_input = together(exchange(stats, CHIPS), next_input)
    next_other = swap(next_input)
    grad_two, partial, mean_one = mixture_call(logits_two, stats, tables, (place, aux))
    partial, next_other = together(partial, next_other)
    pieces = offset_call(exchange(partial, CHIPS), unit, mixed, rms, gain)
    pieces, grad_two = together(exchange(pieces, CHIPS), grad_two)
    two_other = swap(grad_two[block_rows:])

    grad_b, offset_rows, inner, share = first_grad_call(
        place, pieces, logits_one, 1, lse_one, mean_one, aux, tables[1], (next_input, gain)
    )
    one_other = swap(grad_b)
    offset_other = swap(offset_rows)
    share_other = swap(share)
    (grad_a,) = first_grad_call(
        place, offset_rows, logits_one, 0, lse_one, mean_one, aux, tables[0], (inner,)
    )
    head_grad, offset_grad, gain_grad = head_call(
        [
            (grad_two, next_input),
            (two_other, next_other),
            (low, offset_rows),
            (grad_a, hidden),
            (low_other, offset_other),
            (one_other, hidden_other),
        ],
        block_rows,
        place,
        offset_rows,
        offset_other,
        share,
        share_other,
        own_rows,
    )
    return (head_grad, gain_grad.reshape(width), offset_grad)


def solution(mesh):
    fine = Mesh(mesh.devices.reshape(2, 4, 4, 2, 2), ("zh", "y", "x", "zl", "c"))
    rows = DP + VOCAB
    return jax.shard_map(
        local,
        mesh=fine,
        in_specs=(P(DP, None), P(DP, None), P(), P(rows, None), P(), P(), P()),
        out_specs=(P(rows, None), P(), P(DP, None)),
        check_vma=False,
    )
```

time: 230 us -> 224 us (0.974)
  blocking collectives: 143 us -> 170 us
  waiting for transfers between devices: 22.6 us -> 1.16 us
  starting transfers between devices: 18.1 us -> 10.4 us
    all_to_all x6 -> x7, blocking collectives: 143 us -> 170 us  [exchange(): return lax.all_to_all(blocks, axes, 0, 0)]
    all_to_all x1 -> x0, waiting for transfers between devices: 21.5 us -> none  [exchange(): return lax.all_to_all(blocks, axes, 0, 0)]
    all_to_all x1 -> x0, starting transfers between devices: 7.95 us -> none  [exchange(): return lax.all_to_all(blocks, axes, 0, 0)]
    pallas_call x8 -> x9, Pallas kernels: 29.4 us -> 27.8 us  [call(): pl.pallas_call(kernel, in_specs=specs, out_shape=out_shape, out_specs=[wh...]
  transfers between devices with their start and end apart: 9 -> 8, of which waited for: 2 -> 1; matrix products, arithmetic and copies ran while one was open for 1% -> 0% of each run, Pallas kernels for 10% -> 7%
where the time goes in v1:
time: 224 us; the launch traced here: 223 us
  blocking collectives  170 us (76%)
  Pallas kernels  40.7 us (18%)
  starting transfers between devices  10.4 us (5%)
    all_to_all x7, blocking collectives, exchange(): return lax.all_to_all(blocks, axes, 0, 0)  170 us
    pallas_call x9, Pallas kernels, call(): pl.pallas_call(kernel, in_specs=specs, out_shape=out_shape, out_specs=[wh...  27.8 us
    pallas_call x1, Pallas kernels, head_call(): pl.pallas_call(functools.partial(head_kernel, len(pairs)), grid=(block //...  12.9 us
    ppermute x8, starting transfers between devices, swap(): return lax.ppermute(value, 'c', SWAP)  10.4 us
  transfers between devices with their start and end apart: 8, of which 1 were waited for; matrix products, arithmetic and copies ran while one was open for 0% of the time, Pallas kernels for 7%

profile of v1, /device:TPU:1, one launch (start us, length us, event | category | flops | bytes accessed | tf_op | source)
XLA Modules:
  0.0 223.2 jit_solution(13851087054000585527)
XLA Ops:
  0.6 0.1 stack.23.place.refs_0_
  0.7 4.2 %shard_map.94 = (bf16[8,32,3072]{2,1,0:T(8,128)(2,1)S(1)}, f32[4,3072]{1,0:T(4,128)S(1)}, s32[8,256]{1,0:T(8,128)S(1)}, bf16[1024,3072]{1,0:T(8,128)(2,1)S(1)}) custom-call(s32[5]{0:T(128)S(1)} %stack.23.place.refs_0_, bf16[64,3072]{1,0:T(8,128)(2,1)} %hidden.1, bf16[64,3072]{1,0:T(8,128)(2,1)} %offsets.1, s32[4,128]{1,0:T(4,128)} %bitcast.17, ...), custom_call_target="tpu_custom_call" | custom-call | tf_op jit(solution)/shard_map/pallas_call | solution.py:45
  4.9 1.6 collective-permute-start
  6.5 30.3 %all_to_all.35 = bf16[8,32,3072]{2,1,0:T(8,128)(2,1)S(1)} all-to-all(bf16[8,32,3072]{2,1,0:T(8,128)(2,1)S(1)} %get-tuple-element.42), channel_id=1, replica_groups=mesh['zh'=2,'y'=4,'x'=4,'zl'=2,'c'=2] {'zh','y'}, dimensions={0} | all-to-all | bytes 3145728 | tf_op jit(solution)/shard_map/all_to_all | solution.py:29
  36.9 0.8 collective-permute-start.1
  37.7 0.0 collective-permute-done.refs_2_.refs_3_.refs_5_.refs_6_
  37.7 4.0 %shard_map.95 = (f32[2048,256]{1,0:T(8,128)S(1)}, f32[64,2,128]{2,1,0:T(2,128)S(1)}, f32[8,256]{1,0:T(8,128)S(1)}) custom-call(bf16[256,3072]{1,0:T(8,128)(2,1)S(1)} %bitcast.12, bf16[1024,3072]{1,0:T(8,128)(2,1)S(1)} %get-tuple-element.43.refs_1_.refs_2_.refs_4_.refs_6_, bf16[1024,3072]{1,0:T(8,128)(2,1)S(1)} %collective-permute-done.refs_2_.refs_3_.refs_5_.refs_6_), custom_call_target="tpu_custom_call" | custom-call | tf_op jit(solution)/shard_map/pallas_call | solution.py:45
  41.7 0.0 collective-permute-done.1.refs_11_
  41.7 14.4 %all_to_all.36.refs_1_ = f32[64,2,128]{2,1,0:T(2,128)S(1)} all-to-all(f32[64,2,128]{2,1,0:T(2,128)S(1)} %get-tuple-element.46), channel_id=1, replica_groups=mesh['zh'=2,'y'=4,'x'=4,'zl'=2,'c'=2] {'zh','y','x','zl'}, dimensions={0} | all-to-all | bytes 131072 | tf_op jit(solution)/shard_map/all_to_all | solution.py:29
  56.1 3.5 %shard_map.96 = (bf16[2048,256]{1,0:T(8,128)(2,1)S(1)}, bf16[64,4,3072]{2,1,0:T(4,128)(2,1)S(1)}, f32[8,256]{1,0:T(8,128)S(1)}) custom-call(f32[2048,256]{1,0:T(8,128)S(1)} %get-tuple-element.44.refs_0_.refs_2_, f32[64,2,128]{2,1,0:T(2,128)S(1)} %all_to_all.36.refs_1_, bf16[1024,3072]{1,0:T(8,128)(2,1)S(1)} %get-tuple-element.43.refs_1_.refs_2_.refs_4_.refs_6_, ...), custom_call_target="tpu_custom_call" | custom-call | tf_op jit(solution)/shard_map/pallas_call | solution.py:45
  59.7 0.0 copy-start
  59.7 26.0 %all_to_all.37.parts = bf16[64,4,3072]{2,1,0:T(4,128)(2,1)S(1)} all-to-all(bf16[64,4,3072]{2,1,0:T(4,128)(2,1)S(1)} %get-tuple-element.47), channel_id=1, replica_groups=mesh['zh'=2,'y'=4,'x'=4,'zl'=2,'c'=2] {'zh','y','x','zl'}, dimensions={0} | all-to-all | bytes 3145728 | tf_op jit(solution)/shard_map/all_to_all | solution.py:29
  85.7 0.4 shard_map.97
  86.2 28.0 %all_to_all.38.refs_0_ = bf16[64,4,3072]{2,1,0:T(4,128)(2,1)S(1)} all-to-all(bf16[64,4,3072]{2,1,0:T(4,128)(2,1)S(1)} %get-tuple-element.49), channel_id=1, replica_groups=mesh['zh'=2,'y'=4,'x'=4,'zl'=2,'c'=2] {'zh','y','x','zl'}, dimensions={0} | all-to-all | bytes 3145728 | tf_op jit(solution)/shard_map/all_to_all | solution.py:29
  114.2 3.1 %collective-permute-start.2 = (bf16[1024,256]{1,0:T(8,128)(2,1)S(1)}, bf16[1024,256]{1,0:T(8,128)(2,1)S(1)}, u32[]{:S(2)}, u32[]{:S(2)}) collective-permute-start(bf16[1024,256]{1,0:T(8,128)(2,1)S(1)} %slice.6), channel_id=1, source_target_pairs={{0,1},{1,0},{2,3},{3,2},{4,5},{5,4},{6,7},{7,6},{8,9},{9,8},{10,11... | collective-permute-start | bytes 1572872 | tf_op jit(solution)/shard_map/ppermute | solution.py:25
  117.3 4.0 %shard_map.98 = (f32[2048,256]{1,0:T(8,128)S(1)}, f32[64,8,128]{2,1,0:T(8,128)S(1)}, bf16[256,3072]{1,0:T(8,128)(2,1)S(1)}) custom-call(bf16[64,4,3072]{2,1,0:T(4,128)(2,1)S(1)} %all_to_all.38.refs_0_, bf16[1024,3072]{1,0:T(8,128)(2,1)S(1)} %get-tuple-element.43.refs_1_.refs_2_.refs_4_.refs_6_, ...), custom_call_target="tpu_custom_call" | custom-call | tf_op jit(solution)/shard_map/pallas_call | solution.py:45
  121.3 15.6 %all_to_all.39.refs_2_ = f32[64,8,128]{2,1,0:T(8,128)S(1)} all-to-all(f32[64,8,128]{2,1,0:T(8,128)S(1)} %get-tuple-element.57), channel_id=1, replica_groups=mesh['zh'=2,'y'=4,'x'=4,'zl'=2,'c'=2] {'zh','y','x','zl'}, dimensions={0} | all-to-all | bytes 524288 | tf_op jit(solution)/shard_map/all_to_all | solution.py:29
  137.0 1.4 collective-permute-start.3
  138.3 4.6 %shard_map.99 = (bf16[2048,256]{1,0:T(8,128)(2,1)S(1)}, bf16[64,4,3072]{2,1,0:T(4,128)(2,1)S(1)}, f32[8,256]{1,0:T(8,128)S(1)}) custom-call(s32[5]{0:T(128)S(1)} %stack.23.place.refs_0_, f32[2048,256]{1,0:T(8,128)S(1)} %get-tuple-element.54.refs_1_, f32[64,8,128]{2,1,0:T(8,128)S(1)} %all_to_all.39.refs_2_, s32[8,256]{1,0:T(8,128)S(1)} %get-tuple-element.60.refs_3_.refs_5_, ...), custom_call_target="tpu_custom_call" | custom-call | tf_op jit(solution)/shard_map/pallas_call | solution.py:45
  143.0 27.5 %all_to_all.40.parts = bf16[64,4,3072]{2,1,0:T(4,128)(2,1)S(1)} all-to-all(bf16[64,4,3072]{2,1,0:T(4,128)(2,1)S(1)} %get-tuple-element.63), channel_id=1, replica_groups=mesh['zh'=2,'y'=4,'x'=4,'zl'=2,'c'=2] {'zh','y','x','zl'}, dimensions={0} | all-to-all | bytes 3145728 | tf_op jit(solution)/shard_map/all_to_all | solution.py:29
  170.5 0.5 shard_map.100
  171.1 28.1 %all_to_all.41.refs_1_ = bf16[64,4,3200]{2,1,0:T(4,128)(2,1)S(1)} all-to-all(bf16[64,4,3200]{2,1,0:T(4,128)(2,1)S(1)} %shard_map.100), channel_id=1, replica_groups=mesh['zh'=2,'y'=4,'x'=4,'zl'=2,'c'=2] {'zh','y','x','zl'}, dimensions={0} | all-to-all | bytes 3276800 | tf_op jit(solution)/shard_map/all_to_all | solution.py:29
  199.2 3.7 %shard_map.101 = (bf16[1024,256]{1,0:T(8,128)(2,1)S(1)}, bf16[256,3072]{1,0:T(8,128)(2,1)S(1)}, f32[8,256]{1,0:T(8,128)S(1)}, f32[1,3072]{1,0:T(1,128)S(1)}) custom-call(s32[5]{0:T(128)S(1)} %stack.23.place.refs_0_, bf16[64,4,3200]{2,1,0:T(4,128)(2,1)S(1)} %all_to_all.41.refs_1_, f32[2048,256]{1,0:T(8,128)S(1)} %get-tuple-element.44.refs_0_.refs_2_, ...), custom_call_target="tpu_custom_call" | custom-call | tf_op jit(solution)/shard_map/pallas_call | solution.py:45
  202.9 2.9 %collective-permute-start.6 = (bf16[256,3072]{1,0:T(8,128)(2,1)S(1)}, bf16[256,3072]{1,0:T(8,128)(2,1)S(1)}, u32[]{:S(2)}, u32[]{:S(2)}) collective-permute-start(bf16[256,3072]{1,0:T(8,128)(2,1)S(1)} %get-tuple-element.71.refs_1_.refs_8_.refs_12_), channel_id=1, source_target_pairs={{0,1},{1,0},{2,3},{3,2},{4,5},{5,4},{6,7},{7,6},{8,9},{9,8},{10,11... | collective-permute-start | bytes 4718600 | tf_op jit(solution)/shard_map/ppermute | solution.py:25
  205.8 0.1 collective-permute-start.4
  205.9 0.5 collective-permute-start.5
  206.4 0.1 collective-permute-start.7
  206.5 2.7 %shard_map.102.refs_3_ = bf16[1024,256]{1,0:T(8,128)(2,1)S(1)} custom-call(s32[5]{0:T(128)S(1)} %stack.23.place.refs_0_, bf16[256,3072]{1,0:T(8,128)(2,1)S(1)} %get-tuple-element.71.refs_1_.refs_8_.refs_12_, f32[2048,256]{1,0:T(8,128)S(1)} %get-tuple-element.44.refs_0_.refs_2_, f32[8,256]{1,0:T(8,128)S(1)} %get-tuple-element.52.refs_3_, ...), custom_call_target="tpu_custom_call" | custom-call | tf_op jit(solution)/shard_map/pallas_call | solution.py:45
  209.2 1.1 collective-permute-done.7.refs_15_
  210.3 0.0 collective-permute-done.4.refs_1_
  210.3 0.0 collective-permute-done.5.refs_5_
  210.3 12.9 %shard_map.103 = (f32[1024,3072]{1,0:T(8,128)}, bf16[64,3072]{1,0:T(8,128)(2,1)}, f32[1,3072]{1,0:T(1,128)}) custom-call(s32[5]{0:T(128)S(1)} %stack.23.place.refs_0_, bf16[2048,256]{1,0:T(8,128)(2,1)S(1)} %get-tuple-element.68.refs_0_, bf16[1024,256]{1,0:T(8,128)(2,1)S(1)} %collective-permute-done.4.refs_1_, ...), custom_call_target="tpu_custom_call" | custom-call | tf_op jit(solution)/shard_map/pallas_call | solution.py:417
  (6 shorter events, 0.1 us)
Async XLA Ops:
  4.9 32.8 %collective-permute-start = (bf16[1024,3072]{1,0:T(8,128)(2,1)S(1)}, bf16[1024,3072]{1,0:T(8,128)(2,1)S(1)}, u32[]{:S(2)}, u32[]{:S(2)}) collective-permute-start(bf16[1024,3072]{1,0:T(8,128)(2,1)S(1)} %get-tuple-element.43.refs_1_.refs_2_.refs_4_.refs_6_), channel_id=1, source_target_pairs={{0,1},{1,0},{2,3},{3,2},{4,5},{5,4},{6,7},{7,6},{8,9},{9,8},{10,11... | collective-permute-start | bytes 18874376 | tf_op jit(solution)/shard_map/ppermute | solution.py:25
  36.9 4.8 %collective-permute-start.1 = (bf16[256,3072]{1,0:T(8,128)(2,1)S(1)}, bf16[256,3072]{1,0:T(8,128)(2,1)S(1)}, u32[]{:S(2)}, u32[]{:S(2)}) collective-permute-start(bf16[256,3072]{1,0:T(8,128)(2,1)S(1)} %bitcast.11), channel_id=1, source_target_pairs={{0,1},{1,0},{2,3},{3,2},{4,5},{5,4},{6,7},{7,6},{8,9},{9,8},{10,11... | collective-permute-start | bytes 4718600 | tf_op jit(solution)/shard_map/ppermute | solution.py:25
  59.7 26.1 %copy-start = (f32[3072]{0:T(1024)S(1)}, f32[3072]{0:T(1024)}, u32[]{:S(2)}) copy-start(f32[3072]{0:T(1024)} %param.9) | copy-start | bytes 36868
  114.2 7.1 %collective-permute-start.2 = (bf16[1024,256]{1,0:T(8,128)(2,1)S(1)}, bf16[1024,256]{1,0:T(8,128)(2,1)S(1)}, u32[]{:S(2)}, u32[]{:S(2)}) collective-permute-start(bf16[1024,256]{1,0:T(8,128)(2,1)S(1)} %slice.6), channel_id=1, source_target_pairs={{0,1},{1,0},{2,3},{3,2},{4,5},{5,4},{6,7},{7,6},{8,9},{9,8},{10,11... | collective-permute-start | bytes 1572872 | tf_op jit(solution)/shard_map/ppermute | solution.py:25
  137.0 6.0 %collective-permute-start.3 = (bf16[256,3072]{1,0:T(8,128)(2,1)S(1)}, bf16[256,3072]{1,0:T(8,128)(2,1)S(1)}, u32[]{:S(2)}, u32[]{:S(2)}) collective-permute-start(bf16[256,3072]{1,0:T(8,128)(2,1)S(1)} %get-tuple-element.62.refs_7_.refs_6_), channel_id=1, source_target_pairs={{0,1},{1,0},{2,3},{3,2},{4,5},{5,4},{6,7},{7,6},{8,9},{9,8},{10,11... | collective-permute-start | bytes 4718600 | tf_op jit(solution)/shard_map/ppermute | solution.py:25
  202.9 7.4 %collective-permute-start.6 = (bf16[256,3072]{1,0:T(8,128)(2,1)S(1)}, bf16[256,3072]{1,0:T(8,128)(2,1)S(1)}, u32[]{:S(2)}, u32[]{:S(2)}) collective-permute-start(bf16[256,3072]{1,0:T(8,128)(2,1)S(1)} %get-tuple-element.71.refs_1_.refs_8_.refs_12_), channel_id=1, source_target_pairs={{0,1},{1,0},{2,3},{3,2},{4,5},{5,4},{6,7},{7,6},{8,9},{9,8},{10,11... | collective-permute-start | bytes 4718600 | tf_op jit(solution)/shard_map/ppermute | solution.py:25
  205.8 4.5 %collective-permute-start.4 = (bf16[1024,256]{1,0:T(8,128)(2,1)S(1)}, bf16[1024,256]{1,0:T(8,128)(2,1)S(1)}, u32[]{:S(2)}, u32[]{:S(2)}) collective-permute-start(bf16[1024,256]{1,0:T(8,128)(2,1)S(1)} %slice.7), channel_id=1, source_target_pairs={{0,1},{1,0},{2,3},{3,2},{4,5},{5,4},{6,7},{7,6},{8,9},{9,8},{10,11... | collective-permute-start | bytes 1572872 | tf_op jit(solution)/shard_map/ppermute | solution.py:25
  205.9 4.4 %collective-permute-start.5 = (bf16[1024,256]{1,0:T(8,128)(2,1)S(1)}, bf16[1024,256]{1,0:T(8,128)(2,1)S(1)}, u32[]{:S(2)}, u32[]{:S(2)}) collective-permute-start(bf16[1024,256]{1,0:T(8,128)(2,1)S(1)} %get-tuple-element.74), channel_id=1, source_target_pairs={{0,1},{1,0},{2,3},{3,2},{4,5},{5,4},{6,7},{7,6},{8,9},{9,8},{10,11... | collective-permute-start | bytes 1572872 | tf_op jit(solution)/shard_map/ppermute | solution.py:25
  206.4 3.9 %collective-permute-start.7 = (f32[1,3072]{1,0:T(1,128)S(1)}, f32[1,3072]{1,0:T(1,128)S(1)}, u32[]{:S(2)}, u32[]{:S(2)}) collective-permute-start(f32[1,3072]{1,0:T(1,128)S(1)} %get-tuple-element.77.refs_14_), channel_id=1, source_target_pairs={{0,1},{1,0},{2,3},{3,2},{4,5},{5,4},{6,7},{7,6},{8,9},{9,8},{10,11... | collective-permute-start | bytes 36872 | tf_op jit(solution)/shard_map/ppermute | solution.py:25

commit v2 on v1

--- a/solution.py
+++ b/solution.py
@@ -53,9 +53,8 @@
 
 
 def gather_rows(pieces_ref, rows_ref):
-    width = rows_ref.shape[1]
     for j in range(rows_ref.shape[0] // 16):
-        part = [pieces_ref[4 * j + k, :, :width].astype(f32) for k in range(4)]
+        part = [pieces_ref[4 * j + k].astype(f32) for k in range(4)]
         rows_ref[16 * j : 16 * j + 16, :] = jnp.concatenate(part, axis=0).astype(bf16)
 
 
@@ -137,10 +136,10 @@
 
 def logits_kernel(second, *refs):
     if second:
-        pieces, own, other, lse, before, logits, stats, hidden = refs
+        pieces, own, other, logits, stats, hidden = refs
         gather_rows(pieces, hidden)
     else:
-        hidden, own, other, logits, stats, local_out = refs
+        hidden, own, other, logits, stats = refs
     n_rows = logits.shape[1]
     block = other.shape[0]
     old = jnp.full((1, n_rows), -1e30, f32)
@@ -159,44 +158,24 @@
             )
             total = scale * total + jnp.sum(expo, axis=0, keepdims=True)
             old = top
-    log_total = old + jnp.log(total)
-    mean = old + weighted / total
-    lines = in_lines(log_total)
+    lines = in_lines(old + jnp.log(total)) + in_lines(old + weighted / total)
+    stats[...] = jnp.broadcast_to(jnp.concatenate(lines, axis=0)[None], stats.shape)
+
+
+def logits_call(hidden, tables, n_chip):
+    block, width = tables[0].shape
+    second = hidden.ndim == 3
+    rows = hidden.size // width
+    out_shape = [
+        pltpu.VMEM((2 * block, rows), f32),
+        jax.ShapeDtypeStruct((n_chip, 2 * rows // LANES, LANES), f32),
+    ]
     if second:
-        lines += in_lines(mean)
-        lines += in_lines(jnp.exp(before[0:1, :] - lse[0:1, :]) * before[1:2, :])
-    else:
-        local_out[...] = jnp.concatenate([log_total, mean] + [mean] * 6, axis=0)
-    lines += [jnp.zeros((1, LANES), f32)] * (stats.shape[1] - len(lines))
-    stats[...] = jnp.broadcast_to(jnp.concatenate(lines, axis=0)[None], stats.shape)
-
-
-def first_logits_call(hidden, table, other, n_chip):
-    block, width = table.shape
-    rows = hidden.shape[0]
-    return call(
-        functools.partial(logits_kernel, False),
-        [hidden, in_vmem(table), in_vmem(other)],
-        [
-            pltpu.VMEM((2 * block, rows), f32),
-            jax.ShapeDtypeStruct((n_chip, rows // LANES, LANES), f32),
-            jax.ShapeDtypeStruct((8, rows), f32),
-        ],
-    )
-
-
-def second_logits_call(pieces, tables, lse, before):
-    block, width = tables[0].shape
-    n_chip, piece, _ = pieces.shape
-    rows = n_chip * piece
-    return call(
-        functools.partial(logits_kernel, True),
-        [pieces, in_vmem(tables[0]), in_vmem(tables[1]), lse, before],
-        [
-            pltpu.VMEM((2 * block, rows), f32),
-            jax.ShapeDtypeStruct((n_chip, 8, LANES), f32),
-            jax.ShapeDtypeStruct((rows, width), bf16),
-        ],
+        out_shape.append(jax.ShapeDtypeStruct((rows, width), bf16))
+    return call(
+        functools.partial(logits_kernel, second),
+        [hidden, in_vmem(tables[0]), in_vmem(tables[1])],
+        out_shape,
     )
 
 
@@ -222,20 +201,19 @@
 def mixture_kernel(with_grad, *refs):
     if with_grad:
         place, logits, stats, aux, own, other = refs[:6]
+        coef, partial, turned = refs[6:]
     else:
-        logits, stats, own, other = refs[:4]
-    coef, partial, rows, turned = refs[-4:]
+        logits, stats, own, other, coef, partial, rows, turned = refs
     block, width = own.shape
     n_rows = logits.shape[1]
     local_lse = stat(stats, 0, n_rows)
     lse = all_lse(local_lse)
-    row = lse
+    weight = jnp.exp(local_lse - lse)
+    mean = jnp.sum(weight * stat(stats, 1, n_rows), axis=0, keepdims=True)
     if with_grad:
         adv = aux[2:3, :].astype(f32)
-        weight = jnp.exp(local_lse - lse)
-        mean = jnp.sum(weight * stat(stats, 1, n_rows), axis=0, keepdims=True)
-        row = jnp.sum(stat(stats, 2, n_rows), axis=0, keepdims=True)
-    rows[...] = jnp.broadcast_to(row, rows.shape)
+    else:
+        rows[...] = jnp.concatenate([lse] + [mean] * 7, axis=0)
     for start in range(0, 2 * block, VOCAB_TILE):
         tile = logits[start : start + VOCAB_TILE, :]
         probs = jnp.exp(tile - lse)
@@ -256,17 +234,19 @@
     n_rows = logits.shape[1]
     tables = [in_vmem(t) for t in tables]
     operands = [in_vmem(logits), stats, *tables]
-    if grad is not None:
+    out_shape = [
+        jax.ShapeDtypeStruct((2 * block, n_rows), bf16),
+        jax.ShapeDtypeStruct((n_rows // 4, 4, width), bf16),
+    ]
+    if grad is None:
+        out_shape.append(jax.ShapeDtypeStruct((8, n_rows), f32))
+    else:
         place, aux = grad
         operands = [place, in_vmem(logits), stats, aux, *tables]
     return call(
         functools.partial(mixture_kernel, grad is not None),
         operands,
-        [
-            jax.ShapeDtypeStruct((2 * block, n_rows), bf16),
-            jax.ShapeDtypeStruct((n_rows // 4, 4, width), bf16),
-            jax.ShapeDtypeStruct((8, n_rows), f32),
-        ],
+        out_shape,
         [pltpu.VMEM((n_rows, 2 * block), bf16)],
         0 if grad is None else 1,
     )
@@ -336,72 +316,79 @@
     )[0]
 
 
-def first_grad_kernel(half, assemble, *refs):
-    if assemble:
-        place, pieces, logits, lse, mean, aux, table, next_input, gain = refs[:9]
-        grad, hidden, inner_out, share = refs[9:]
-        n_rows, width = hidden.shape
-        gather_rows(pieces, hidden)
-        terms = [pieces[k, :, width:].astype(f32) for k in range(pieces.shape[0])]
-        terms = jnp.concatenate(terms, axis=0)
-        inner = terms.T
-        inner = inner[0:1, :] + inner[1:2, :] + inner[2:3, :]
-        inner_out[...] = jnp.broadcast_to(inner, inner_out.shape)
-        along = terms[:, 3:4] + terms[:, 4:5] + terms[:, 5:6]
-        rms = terms[:, 6:7] + terms[:, 7:8] + terms[:, 8:9]
-        for start in range(0, width, WIDTH_TILE):
-            columns = slice(start, start + WIDTH_TILE)
-            given = next_input[:, columns].astype(f32)
-            inverse = 1.0 / gain[:, columns]
-            value = hidden[:, columns].astype(f32) * rms + given * inverse * along
-            value = jnp.sum(value * given, axis=0, keepdims=True)
-            share[:, columns] = value * inverse * inverse
-    else:
-        place, hidden, logits, lse, mean, aux, table, inner_in, grad = refs
-        inner = inner_in[0:1, :]
-    block = table.shape[0]
+def rows_kernel(pieces, next_input, gain, hidden, inner_out, share):
+    gather_rows(pieces, hidden)
+    width = share.shape[1]
+    inner = hidden[:, width:].astype(f32).T
+    inner = inner[0:1, :] + inner[1:2, :] + inner[2:3, :]
+    inner_out[...] = jnp.broadcast_to(inner, inner_out.shape)
+    for start in range(0, width, WIDTH_TILE):
+        columns = slice(start, start + WIDTH_TILE)
+        share[:, columns] = gain_share(hidden, next_input, gain, columns, width)
+
+
+def rows_call(pieces, next_input, gain):
+    n_rows, width = next_input.shape
+    return call(
+        rows_kernel,
+        [pieces, next_input, gain],
+        [
+            jax.ShapeDtypeStruct((n_rows, pieces.shape[2]), bf16),
+            jax.ShapeDtypeStruct((8, n_rows), f32),
+            jax.ShapeDtypeStruct((1, width), f32),
+        ],
+    )
+
+
+def first_grad_kernel(half, place, hidden, logits, rows, aux, table, inner_in, grad):
+    inner = inner_in[0:1, :]
+    block, width = table.shape
     adv = aux[2:3, :].astype(f32)
+    lse, mean = rows[0:1, :], rows[1:2, :]
     for start in range(0, block, VOCAB_TILE):
-        prob_grad = nt(table[start : start + VOCAB_TILE, :], hidden[...])
+        prob_grad = nt(table[start : start + VOCAB_TILE, :], hidden[:, :width])
         tile = logits[half * block + start : half * block + start + VOCAB_TILE, :]
-        probs = jnp.exp(tile - lse[0:1, :])
+        probs = jnp.exp(tile - lse)
         entries = entries_of(place[half] + start, *tile.shape)
-        value = logit_grad(tile, probs, mean[0:1, :], adv, entries, aux[0:1, :])
+        value = logit_grad(tile, probs, mean, adv, entries, aux[0:1, :])
         value = value + probs * (prob_grad - inner)
         grad[start : start + VOCAB_TILE, :] = value.astype(bf16)
 
 
-def first_grad_call(place, hidden, logits, half, lse, mean, aux, table, more):
-    block, width = table.shape
-    n_rows = logits.shape[1]
-    out_shape = [jax.ShapeDtypeStruct((block, n_rows), bf16)]
-    operands = [place, hidden, in_vmem(logits), lse, mean, aux, in_vmem(table), *more]
-    assemble = hidden.ndim == 3
-    if assemble:
-        out_shape += [
-            jax.ShapeDtypeStruct((n_rows, width), bf16),
-            jax.ShapeDtypeStruct((8, n_rows), f32),
-            jax.ShapeDtypeStruct((1, width), f32),
-        ]
-    return call(
-        functools.partial(first_grad_kernel, half, assemble), operands, out_shape, (), 1
-    )
+def first_grad_call(place, hidden, logits, half, rows, aux, table, inner):
+    return call(
+        functools.partial(first_grad_kernel, half),
+        [place, hidden, in_vmem(logits), rows, aux, in_vmem(table), inner],
+        [jax.ShapeDtypeStruct((table.shape[0], logits.shape[1]), bf16)],
+        (),
+        1,
+    )[0]
+
+
+def gain_share(offset_rows, next_input, gain, columns, width):
+    terms = offset_rows[:, width:].astype(f32)
+    along = terms[:, 3:4] + terms[:, 4:5] + terms[:, 5:6]
+    rms = terms[:, 6:7] + terms[:, 7:8] + terms[:, 8:9]
+    given = next_input[:, columns].astype(f32)
+    inverse = 1.0 / gain[:, columns]
+    value = offset_rows[:, columns].astype(f32) * rms + given * inverse * along
+    return jnp.sum(value * given, axis=0, keepdims=True) * inverse * inverse
 
 
 def head_kernel(n, place, *refs):
     lefts, rights = refs[:n], refs[n : 2 * n]
-    mine, theirs, gain_a, gain_b, head, offset, gain = refs[2 * n :]
+    mine, theirs, share, share_other, head, offset, gain_grad = refs[2 * n :]
+    tile, width = head.shape
 
     @pl.when(pl.program_id(0) == 0)
     def _():
-        gain[...] = gain_a[...] + gain_b[...]
+        gain_grad[...] = share[...] + share_other[...]
         half = offset.shape[0] // 2
         at = pl.ds(pl.multiple_of(place[2] * half, half), half)
         low = place[3] == 0
-        offset[:half, :] = jnp.where(low, mine[at, :], theirs[at, :])
-        offset[half:, :] = jnp.where(low, theirs[at, :], mine[at, :])
-
-    tile, width = head.shape
+        offset[:half, :] = jnp.where(low, mine[at, :width], theirs[at, :width])
+        offset[half:, :] = jnp.where(low, theirs[at, :width], mine[at, :width])
+
     row = pl.ds(pl.multiple_of(pl.program_id(0) * tile, tile), tile)
     left = jnp.concatenate([r[row, :] for r in lefts], axis=1)
     for start in range(0, width, WIDTH_TILE):
@@ -410,10 +397,9 @@
         head[:, columns] = jnp.dot(left, right, preferred_element_type=f32)
 
 
-def head_call(pairs, block, place, offset_rows, offset_other, gain_a, gain_b, own_rows):
+def head_call(pairs, block, place, more, own_rows):
     width = pairs[0][1].shape[1]
-    operands = [p[0] for p in pairs] + [p[1] for p in pairs]
-    operands += [offset_rows, offset_other, gain_a, gain_b]
+    operands = [p[0] for p in pairs] + [p[1] for p in pairs] + list(more)
     return pl.pallas_call(
         functools.partial(head_kernel, len(pairs)),
         grid=(block // HEAD_TILE,),
@@ -421,7 +407,7 @@
         out_shape=[
             jax.ShapeDtypeStruct((block, width), f32),
             jax.ShapeDtypeStruct((own_rows, width), bf16),
-            jax.ShapeDtypeStruct(gain_a.shape, f32),
+            jax.ShapeDtypeStruct((1, width), f32),
         ],
         out_specs=[pl.BlockSpec((HEAD_TILE, width), lambda i: (i, 0)), whole(), whole()],
         compiler_params=pltpu.CompilerParams(vmem_limit_bytes=24 * 1024 * 1024),
@@ -447,35 +433,35 @@
     own_half, own_offsets, aux, own = start_call(
         place, start_hidden, offsets, targets_one, targets_two, advantage, head_table, n_dp, piece
     )
-    other = swap(own)
+    tables = (own, swap(own))
     hidden = exchange(own_half, DP).reshape(rows, width)
+    logits_one, stats = logits_call(hidden, tables, n_chip)
+    low, partial, rows_one = mixture_call(logits_one, exchange(stats, CHIPS), tables)
+    pieces, unit, mixed, rms = state_call(exchange(partial, CHIPS), own_offsets, gain)
+
+    pieces, low, hidden = together(exchange(pieces, CHIPS), low, hidden)
+    low_other = swap(low[block_rows:])
     hidden_other = swap(hidden)
-    logits_one, stats, before = first_logits_call(hidden, own, other, n_chip)
-    tables = (own, other)
-    stats, hidden_other = together(stats, hidden_other)
-    low, partial, lse_one = mixture_call(logits_one, exchange(stats, CHIPS), tables)
-    pieces, unit, mixed, rms = state_call(exchange(partial, CHIPS), own_offsets, gain)
-
-    pieces, low = together(exchange(pieces, CHIPS), low)
-    low_other = swap(low[block_rows:])
-    logits_two, stats, next_input = second_logits_call(pieces, tables, lse_one, before)
-    stats, low_other = together(stats, low_other)
-    stats, next_input = together(exchange(stats, CHIPS), next_input)
+    logits_two, stats, next_input = logits_call(pieces, tables, n_chip)
+    stats, low_other, hidden_other = together(stats, low_other, hidden_other)
+    grad_two, partial = mixture_call(
+        logits_two, exchange(stats, CHIPS), tables, (place, aux)
+    )
+    pieces = offset_call(exchange(partial, CHIPS), unit, mixed, rms, gain)
+    pieces, grad_two, next_input = together(exchange(pieces, CHIPS), grad_two, next_input)
     next_other = swap(next_input)
-    grad_two, partial, mean_one = mixture_call(logits_two, stats, tables, (place, aux))
-    partial, next_other = together(partial, next_other)
-    pieces = offset_call(exchange(partial, CHIPS), unit, mixed, rms, gain)
-    pieces, grad_two = together(exchange(pieces, CHIPS), grad_two)
     two_other = swap(grad_two[block_rows:])
 
-    grad_b, offset_rows, inner, share = first_grad_call(
-        place, pieces, logits_one, 1, lse_one, mean_one, aux, tables[1], (next_input, gain)
-    )
-    one_other = swap(grad_b)
+    offset_rows, inner, share = rows_call(pieces, next_input, gain)
     offset_other = swap(offset_rows)
     share_other = swap(share)
-    (grad_a,) = first_grad_call(
-        place, offset_rows, logits_one, 0, lse_one, mean_one, aux, tables[0], (inner,)
+    grad_b = first_grad_call(
+        place, offset_rows, logits_one, 1, rows_one, aux, tables[1], inner
+    )
+    one_other = swap(grad_b)
+    inner, offset_other = together(inner, offset_other)
+    grad_a = first_grad_call(
+        place, offset_rows, logits_one, 0, rows_one, aux, tables[0], inner
     )
     head_grad, offset_grad, gain_grad = head_call(
         [
@@ -488,10 +474,7 @@
         ],
         block_rows,
         place,
-        offset_rows,
-        offset_other,
-        share,
-        share_other,
+        (offset_rows, offset_other, share, share_other),
         own_rows,
     )
     return (head_grad, gain_grad.reshape(width), offset_grad)

time: 224 us -> 219 us (0.978)
  blocking collectives: 170 us -> 165 us
    all_to_all x7, blocking collectives: 170 us -> 165 us  [exchange(): return lax.all_to_all(blocks, axes, 0, 0)]
    pallas_call x9 -> x10, Pallas kernels: 27.8 us -> 28.2 us  [call(): pl.pallas_call(kernel, in_specs=specs, out_shape=out_shape, out_specs=[wh...]
  transfers between devices with their start and end apart: 8 -> 8, of which waited for: 1 -> 1; matrix products, arithmetic and copies ran while one was open for 0% -> 0% of each run, Pallas kernels for 7% -> 4%
where the time goes in v2:
time: 219 us; the launch traced here: 218 us
  blocking collectives  165 us (75%)
  Pallas kernels  41.2 us (19%)
  starting transfers between devices  11 us (5%)
    all_to_all x7, blocking collectives, exchange(): return lax.all_to_all(blocks, axes, 0, 0)  165 us
    pallas_call x10, Pallas kernels, call(): pl.pallas_call(kernel, in_specs=specs, out_shape=out_shape, out_specs=[wh...  28.2 us
    pallas_call x1, Pallas kernels, head_call(): pl.pallas_call(functools.partial(head_kernel, len(pairs)), grid=(block //...  12.9 us
    ppermute x8, starting transfers between devices, swap(): return lax.ppermute(value, 'c', SWAP)  11 us
  transfers between devices with their start and end apart: 8, of which 1 were waited for; matrix products, arithmetic and copies ran while one was open for 0% of the time, Pallas kernels for 4%

profile of v2, /device:TPU:1, one launch (start us, length us, event | category | flops | bytes accessed | tf_op | source)
XLA Modules:
  0.0 218.4 jit_solution(8446959890466157770)
XLA Ops:
  0.6 0.1 stack.23.place.refs_0_
  0.7 4.2 %shard_map.94 = (bf16[8,32,3072]{2,1,0:T(8,128)(2,1)S(1)}, f32[4,3072]{1,0:T(4,128)S(1)}, s32[8,256]{1,0:T(8,128)S(1)}, bf16[1024,3072]{1,0:T(8,128)(2,1)S(1)}) custom-call(s32[5]{0:T(128)S(1)} %stack.23.place.refs_0_, bf16[64,3072]{1,0:T(8,128)(2,1)} %hidden.1, bf16[64,3072]{1,0:T(8,128)(2,1)} %offsets.1, s32[4,128]{1,0:T(4,128)} %bitcast.17, ...), custom_call_target="tpu_custom_call" | custom-call | tf_op jit(solution)/shard_map/pallas_call | solution.py:45
  4.9 1.6 collective-permute-start
  6.5 30.3 %all_to_all.35 = bf16[8,32,3072]{2,1,0:T(8,128)(2,1)S(1)} all-to-all(bf16[8,32,3072]{2,1,0:T(8,128)(2,1)S(1)} %get-tuple-element.38), channel_id=1, replica_groups=mesh['zh'=2,'y'=4,'x'=4,'zl'=2,'c'=2] {'zh','y'}, dimensions={0} | all-to-all | bytes 3145728 | tf_op jit(solution)/shard_map/all_to_all | solution.py:29
  36.9 0.0 collective-permute-done.refs_2_.refs_3_.refs_5_.table
  36.9 4.0 %shard_map.95 = (f32[2048,256]{1,0:T(8,128)S(1)}, f32[64,4,128]{2,1,0:T(4,128)S(1)}) custom-call(bf16[256,3072]{1,0:T(8,128)(2,1)S(1)} %bitcast.11, bf16[1024,3072]{1,0:T(8,128)(2,1)S(1)} %get-tuple-element.39.refs_1_.refs_2_.refs_4_.table, bf16[1024,3072]{1,0:T(8,128)(2,1)S(1)} %collective-permute-done.refs_2_.refs_3_.refs_5_.table), custom_call_target="tpu_custom_call" | custom-call | tf_op jit(solution)/shard_map/pallas_call | solution.py:45
  40.9 14.3 %all_to_all.36.refs_1_ = f32[64,4,128]{2,1,0:T(4,128)S(1)} all-to-all(f32[64,4,128]{2,1,0:T(4,128)S(1)} %get-tuple-element.41), channel_id=1, replica_groups=mesh['zh'=2,'y'=4,'x'=4,'zl'=2,'c'=2] {'zh','y','x','zl'}, dimensions={0} | all-to-all | bytes 262144 | tf_op jit(solution)/shard_map/all_to_all | solution.py:29
  55.2 3.6 %shard_map.96 = (bf16[2048,256]{1,0:T(8,128)(2,1)S(1)}, bf16[64,4,3072]{2,1,0:T(4,128)(2,1)S(1)}, f32[8,256]{1,0:T(8,128)S(1)}) custom-call(f32[2048,256]{1,0:T(8,128)S(1)} %get-tuple-element.40.refs_0_.logits, f32[64,4,128]{2,1,0:T(4,128)S(1)} %all_to_all.36.refs_1_, bf16[1024,3072]{1,0:T(8,128)(2,1)S(1)} %get-tuple-element.39.refs_1_.refs_2_.refs_4_.table, ...), custom_call_target="tpu_custom_call" | custom-call | tf_op jit(solution)/shard_map/pallas_call | solution.py:45
  58.8 0.0 copy-start
  58.8 25.6 %all_to_all.37.parts = bf16[64,4,3072]{2,1,0:T(4,128)(2,1)S(1)} all-to-all(bf16[64,4,3072]{2,1,0:T(4,128)(2,1)S(1)} %get-tuple-element.42), channel_id=1, replica_groups=mesh['zh'=2,'y'=4,'x'=4,'zl'=2,'c'=2] {'zh','y','x','zl'}, dimensions={0} | all-to-all | bytes 3145728 | tf_op jit(solution)/shard_map/all_to_all | solution.py:29
  84.5 0.4 shard_map.97
  84.9 27.1 %all_to_all.38.refs_0_ = bf16[64,4,3072]{2,1,0:T(4,128)(2,1)S(1)} all-to-all(bf16[64,4,3072]{2,1,0:T(4,128)(2,1)S(1)} %get-tuple-element.44), channel_id=1, replica_groups=mesh['zh'=2,'y'=4,'x'=4,'zl'=2,'c'=2] {'zh','y','x','zl'}, dimensions={0} | all-to-all | bytes 3145728 | tf_op jit(solution)/shard_map/all_to_all | solution.py:29
  112.0 3.8 %collective-permute-start.2 = (bf16[256,3072]{1,0:T(8,128)(2,1)S(1)}, bf16[256,3072]{1,0:T(8,128)(2,1)S(1)}, u32[]{:S(2)}, u32[]{:S(2)}) collective-permute-start(bf16[256,3072]{1,0:T(8,128)(2,1)S(1)} %bitcast.12), channel_id=1, source_target_pairs={{0,1},{1,0},{2,3},{3,2},{4,5},{5,4},{6,7},{7,6},{8,9},{9,8},{10,11... | collective-permute-start | bytes 4718600 | tf_op jit(solution)/shard_map/ppermute | solution.py:25
  115.9 0.3 collective-permute-start.1
  116.1 4.0 %shard_map.98 = (f32[2048,256]{1,0:T(8,128)S(1)}, f32[64,4,128]{2,1,0:T(4,128)S(1)}, bf16[256,3072]{1,0:T(8,128)(2,1)S(1)}) custom-call(bf16[64,4,3072]{2,1,0:T(4,128)(2,1)S(1)} %all_to_all.38.refs_0_, bf16[1024,3072]{1,0:T(8,128)(2,1)S(1)} %get-tuple-element.39.refs_1_.refs_2_.refs_4_.table, ...), custom_call_target="tpu_custom_call" | custom-call | tf_op jit(solution)/shard_map/pallas_call | solution.py:45
  120.2 0.0 collective-permute-done.1.refs_4_
  120.2 14.4 %all_to_all.39.refs_2_ = f32[64,4,128]{2,1,0:T(4,128)S(1)} all-to-all(f32[64,4,128]{2,1,0:T(4,128)S(1)} %get-tuple-element.51), channel_id=1, replica_groups=mesh['zh'=2,'y'=4,'x'=4,'zl'=2,'c'=2] {'zh','y','x','zl'}, dimensions={0} | all-to-all | bytes 262144 | tf_op jit(solution)/shard_map/all_to_all | solution.py:29
  134.5 4.6 %shard_map.99 = (bf16[2048,256]{1,0:T(8,128)(2,1)S(1)}, bf16[64,4,3072]{2,1,0:T(4,128)(2,1)S(1)}) custom-call(s32[5]{0:T(128)S(1)} %stack.23.place.refs_0_, f32[2048,256]{1,0:T(8,128)S(1)} %get-tuple-element.47.refs_1_, f32[64,4,128]{2,1,0:T(4,128)S(1)} %all_to_all.39.refs_2_, s32[8,256]{1,0:T(8,128)S(1)} %get-tuple-element.52.refs_3_.aux, ...), custom_call_target="tpu_custom_call" | custom-call | tf_op jit(solution)/shard_map/pallas_call | solution.py:45
  139.2 26.2 %all_to_all.40.parts = bf16[64,4,3072]{2,1,0:T(4,128)(2,1)S(1)} all-to-all(bf16[64,4,3072]{2,1,0:T(4,128)(2,1)S(1)} %get-tuple-element.53), channel_id=1, replica_groups=mesh['zh'=2,'y'=4,'x'=4,'zl'=2,'c'=2] {'zh','y','x','zl'}, dimensions={0} | all-to-all | bytes 3145728 | tf_op jit(solution)/shard_map/all_to_all | solution.py:29
  165.4 0.5 shard_map.100
  166.0 27.1 %all_to_all.41.pieces = bf16[64,4,3200]{2,1,0:T(4,128)(2,1)S(1)} all-to-all(bf16[64,4,3200]{2,1,0:T(4,128)(2,1)S(1)} %shard_map.100), channel_id=1, replica_groups=mesh['zh'=2,'y'=4,'x'=4,'zl'=2,'c'=2] {'zh','y','x','zl'}, dimensions={0} | all-to-all | bytes 3276800 | tf_op jit(solution)/shard_map/all_to_all | solution.py:29
  193.1 1.5 shard_map.101
  194.6 3.9 %collective-permute-start.4 = (bf16[256,3200]{1,0:T(8,128)(2,1)S(1)}, bf16[256,3200]{1,0:T(8,128)(2,1)S(1)}, u32[]{:S(2)}, u32[]{:S(2)}) collective-permute-start(bf16[256,3200]{1,0:T(8,128)(2,1)S(1)} %get-tuple-element.62.hidden.refs_8_.refs_12_), channel_id=1, source_target_pairs={{0,1},{1,0},{2,3},{3,2},{4,5},{5,4},{6,7},{7,6},{8,9},{9,8},{10,11... | collective-permute-start | bytes 4915208 | tf_op jit(solution)/shard_map/ppermute | solution.py:25
  198.6 0.1 collective-permute-start.6
  198.7 0.7 collective-permute-start.3
  199.4 2.7 %shard_map.103 = bf16[1024,256]{1,0:T(8,128)(2,1)S(1)} custom-call(s32[5]{0:T(128)S(1)} %stack.23.place.refs_0_, bf16[256,3200]{1,0:T(8,128)(2,1)S(1)} %get-tuple-element.62.hidden.refs_8_.refs_12_, f32[2048,256]{1,0:T(8,128)S(1)} %get-tuple-element.40.refs_0_.logits, f32[8,256]{1,0:T(8,128)S(1)} %get-tuple-element.63.rows, ...), custom_call_target="tpu_custom_call" | custom-call | tf_op jit(solution)/shard_map/pallas_call | solution.py:45
  202.1 0.2 collective-permute-start.5
  202.2 0.4 collective-permute-start.7
  202.7 0.0 collective-permute-done.4.refs_10_.refs_13_
  202.7 2.7 %shard_map.102.refs_3_ = bf16[1024,256]{1,0:T(8,128)(2,1)S(1)} custom-call(s32[5]{0:T(128)S(1)} %stack.23.place.refs_0_, bf16[256,3200]{1,0:T(8,128)(2,1)S(1)} %get-tuple-element.62.hidden.refs_8_.refs_12_, f32[2048,256]{1,0:T(8,128)S(1)} %get-tuple-element.40.refs_0_.logits, f32[8,256]{1,0:T(8,128)S(1)} %get-tuple-element.63.rows, ...), custom_call_target="tpu_custom_call" | custom-call | tf_op jit(solution)/shard_map/pallas_call | solution.py:45
  205.3 0.1 collective-permute-done.7.refs_15_
  205.5 12.9 %shard_map.104 = (f32[1024,3072]{1,0:T(8,128)}, bf16[64,3072]{1,0:T(8,128)(2,1)}, f32[1,3072]{1,0:T(1,128)}) custom-call(s32[5]{0:T(128)S(1)} %stack.23.place.refs_0_, bf16[2048,256]{1,0:T(8,128)(2,1)S(1)} %get-tuple-element.59.refs_0_, bf16[1024,256]{1,0:T(8,128)(2,1)S(1)} %collective-permute-done.3.refs_1_, ...), custom_call_target="tpu_custom_call" | custom-call | tf_op jit(solution)/shard_map/pallas_call | solution.py:403
  (7 shorter events, 0.1 us)
Async XLA Ops:
  4.9 32.0 %collective-permute-start = (bf16[1024,3072]{1,0:T(8,128)(2,1)S(1)}, bf16[1024,3072]{1,0:T(8,128)(2,1)S(1)}, u32[]{:S(2)}, u32[]{:S(2)}) collective-permute-start(bf16[1024,3072]{1,0:T(8,128)(2,1)S(1)} %get-tuple-element.39.refs_1_.refs_2_.refs_4_.table), channel_id=1, source_target_pairs={{0,1},{1,0},{2,3},{3,2},{4,5},{5,4},{6,7},{7,6},{8,9},{9,8},{10,11... | collective-permute-start | bytes 18874376 | tf_op jit(solution)/shard_map/ppermute | solution.py:25
  58.8 25.6 %copy-start = (f32[3072]{0:T(1024)S(1)}, f32[3072]{0:T(1024)}, u32[]{:S(2)}) copy-start(f32[3072]{0:T(1024)} %param.9) | copy-start | bytes 36868
  112.0 8.2 %collective-permute-start.2 = (bf16[256,3072]{1,0:T(8,128)(2,1)S(1)}, bf16[256,3072]{1,0:T(8,128)(2,1)S(1)}, u32[]{:S(2)}, u32[]{:S(2)}) collective-permute-start(bf16[256,3072]{1,0:T(8,128)(2,1)S(1)} %bitcast.12), channel_id=1, source_target_pairs={{0,1},{1,0},{2,3},{3,2},{4,5},{5,4},{6,7},{7,6},{8,9},{9,8},{10,11... | collective-permute-start | bytes 4718600 | tf_op jit(solution)/shard_map/ppermute | solution.py:25
  115.9 4.3 %collective-permute-start.1 = (bf16[1024,256]{1,0:T(8,128)(2,1)S(1)}, bf16[1024,256]{1,0:T(8,128)(2,1)S(1)}, u32[]{:S(2)}, u32[]{:S(2)}) collective-permute-start(bf16[1024,256]{1,0:T(8,128)(2,1)S(1)} %slice.6), channel_id=1, source_target_pairs={{0,1},{1,0},{2,3},{3,2},{4,5},{5,4},{6,7},{7,6},{8,9},{9,8},{10,11... | collective-permute-start | bytes 1572872 | tf_op jit(solution)/shard_map/ppermute | solution.py:25
  194.6 8.0 %collective-permute-start.4 = (bf16[256,3200]{1,0:T(8,128)(2,1)S(1)}, bf16[256,3200]{1,0:T(8,128)(2,1)S(1)}, u32[]{:S(2)}, u32[]{:S(2)}) collective-permute-start(bf16[256,3200]{1,0:T(8,128)(2,1)S(1)} %get-tuple-element.62.hidden.refs_8_.refs_12_), channel_id=1, source_target_pairs={{0,1},{1,0},{2,3},{3,2},{4,5},{5,4},{6,7},{7,6},{8,9},{9,8},{10,11... | collective-permute-start | bytes 4915208 | tf_op jit(solution)/shard_map/ppermute | solution.py:25
  198.6 6.9 %collective-permute-start.6 = (bf16[256,3072]{1,0:T(8,128)(2,1)S(1)}, bf16[256,3072]{1,0:T(8,128)(2,1)S(1)}, u32[]{:S(2)}, u32[]{:S(2)}) collective-permute-start(bf16[256,3072]{1,0:T(8,128)(2,1)S(1)} %get-tuple-element.61.next_input.refs_6_), channel_id=1, source_target_pairs={{0,1},{1,0},{2,3},{3,2},{4,5},{5,4},{6,7},{7,6},{8,9},{9,8},{10,11... | collective-permute-start | bytes 4718600 | tf_op jit(solution)/shard_map/ppermute | solution.py:25
  198.7 6.8 %collective-permute-start.3 = (bf16[1024,256]{1,0:T(8,128)(2,1)S(1)}, bf16[1024,256]{1,0:T(8,128)(2,1)S(1)}, u32[]{:S(2)}, u32[]{:S(2)}) collective-permute-start(bf16[1024,256]{1,0:T(8,128)(2,1)S(1)} %slice.7), channel_id=1, source_target_pairs={{0,1},{1,0},{2,3},{3,2},{4,5},{5,4},{6,7},{7,6},{8,9},{9,8},{10,11... | collective-permute-start | bytes 1572872 | tf_op jit(solution)/shard_map/ppermute | solution.py:25
  202.1 3.4 %collective-permute-start.5 = (bf16[1024,256]{1,0:T(8,128)(2,1)S(1)}, bf16[1024,256]{1,0:T(8,128)(2,1)S(1)}, u32[]{:S(2)}, u32[]{:S(2)}) collective-permute-start(bf16[1024,256]{1,0:T(8,128)(2,1)S(1)} %shard_map.103), channel_id=1, source_target_pairs={{0,1},{1,0},{2,3},{3,2},{4,5},{5,4},{6,7},{7,6},{8,9},{9,8},{10,11... | collective-permute-start | bytes 1572872 | tf_op jit(solution)/shard_map/ppermute | solution.py:25
  202.2 3.2 %collective-permute-start.7 = (f32[1,3072]{1,0:T(1,128)S(1)}, f32[1,3072]{1,0:T(1,128)S(1)}, u32[]{:S(2)}, u32[]{:S(2)}) collective-permute-start(f32[1,3072]{1,0:T(1,128)S(1)} %get-tuple-element.69.refs_14_), channel_id=1, source_target_pairs={{0,1},{1,0},{2,3},{3,2},{4,5},{5,4},{6,7},{7,6},{8,9},{9,8},{10,11... | collective-permute-start | bytes 36872 | tf_op jit(solution)/shard_map/ppermute | solution.py:25

commit v3 on v2

--- a/solution.py
+++ b/solution.py
@@ -80,20 +80,22 @@
     spread_out, own_offsets, aux, own, offset_rows, lines, sems = refs[4:]
     low = place[3] == 0
     n_dp, half, _ = spread_out.shape
-    mine = hidden.at[pl.ds(pl.multiple_of(place[3] * half, half), half)]
-    moves = [(mine, spread_out.at[k]) for k in range(n_dp)]
-    moves += [(offsets, offset_rows)] + [(v, lines.at[k]) for k, v in enumerate(given)]
+    mine = pl.ds(pl.multiple_of(place[3] * half, half), half)
+    moves = [(hidden.at[mine], spread_out.at[0]), (offsets.at[mine], offset_rows)]
+    moves += [(v, lines.at[k]) for k, v in enumerate(given)]
     moves += [(table, own)]
     copies = [pltpu.make_async_copy(f, t, sems.at[k]) for k, (f, t) in enumerate(moves)]
     for copy in copies:
         copy.start()
-    for copy in copies[n_dp:-1]:
+    for copy in copies[:-1]:
         copy.wait()
+    for k in range(1, n_dp):
+        spread_out[k] = spread_out[0]
     piece = own_offsets.shape[0]
     values = offset_rows[...].astype(f32)
     chosen = values[:piece]
     for k in range(1, values.shape[0] // piece):
-        chosen = jnp.where(place[4] == k, values[piece * k : piece * (k + 1)], chosen)
+        chosen = jnp.where(place[4] == place[3] * (half // piece) + k, values[piece * k : piece * (k + 1)], chosen)
     own_offsets[...] = chosen
     rows = []
     for k in range(len(given)):
@@ -106,8 +108,7 @@
             parts.append(jnp.where(low, first, second))
         rows.append(jnp.concatenate(parts, axis=1))
     aux[...] = jnp.concatenate(rows + [rows[0]] * 5, axis=0)
-    for copy in copies[:n_dp] + copies[-1:]:
-        copy.wait()
+    copies[-1].wait()
 
 
 def start_call(place, start_hidden, offsets, targets_one, targets_two, advantage, table, n_dp, piece):
@@ -125,9 +126,9 @@
             pltpu.VMEM(table.shape, bf16),
         ],
         [
-            pltpu.VMEM((own_rows, width), bf16),
+            pltpu.VMEM((half, width), bf16),
             pltpu.VMEM((3, *lines[0].shape), jnp.int32),
-            pltpu.SemaphoreType.DMA((n_dp + 5,)),
+            pltpu.SemaphoreType.DMA((6,)),
         ],
         scalars=1,
         far=range(1, 7),

time: 219 us -> 218 us (level)
  no operation moved by 1% of the time
where the time goes in v3:
time: 218 us
  blocking collectives  166 us (76%)
  Pallas kernels  40.6 us (19%)
  starting transfers between devices  10.1 us (5%)
    all_to_all x7, blocking collectives, exchange(): return lax.all_to_all(blocks, axes, 0, 0)  166 us
    pallas_call x10, Pallas kernels, call(): pl.pallas_call(kernel, in_specs=specs, out_shape=out_shape, out_specs=[wh...  27.7 us
    pallas_call x1, Pallas kernels, head_call(): pl.pallas_call(functools.partial(head_kernel, len(pairs)), grid=(block //...  12.9 us
    ppermute x8, starting transfers between devices, swap(): return lax.ppermute(value, 'c', SWAP)  10.1 us
  transfers between devices with their start and end apart: 8, of which 1 were waited for; matrix products, arithmetic and copies ran while one was open for 0% of the time, Pallas kernels for 4%

profile of v3, /device:TPU:1, one launch (start us, length us, event | category | flops | bytes accessed | tf_op | source)
XLA Modules:
  0.0 218.1 jit_solution(3879361039183776047)
XLA Ops:
  0.6 0.1 stack.23.place.refs_0_
  0.7 3.7 %shard_map.94 = (bf16[8,32,3072]{2,1,0:T(8,128)(2,1)S(1)}, f32[4,3072]{1,0:T(4,128)S(1)}, s32[8,256]{1,0:T(8,128)S(1)}, bf16[1024,3072]{1,0:T(8,128)(2,1)S(1)}) custom-call(s32[5]{0:T(128)S(1)} %stack.23.place.refs_0_, bf16[64,3072]{1,0:T(8,128)(2,1)} %hidden.1, bf16[64,3072]{1,0:T(8,128)(2,1)} %offsets.1, s32[4,128]{1,0:T(4,128)} %bitcast.17, ...), custom_call_target="tpu_custom_call" | custom-call | tf_op jit(solution)/shard_map/pallas_call | solution.py:45
  4.4 1.5 collective-permute-start
  5.9 30.3 %all_to_all.35 = bf16[8,32,3072]{2,1,0:T(8,128)(2,1)S(1)} all-to-all(bf16[8,32,3072]{2,1,0:T(8,128)(2,1)S(1)} %get-tuple-element.38), channel_id=1, replica_groups=mesh['zh'=2,'y'=4,'x'=4,'zl'=2,'c'=2] {'zh','y'}, dimensions={0} | all-to-all | bytes 3145728 | tf_op jit(solution)/shard_map/all_to_all | solution.py:29
  36.2 0.0 collective-permute-done.refs_2_.refs_3_.refs_5_.table
  36.2 4.0 %shard_map.95 = (f32[2048,256]{1,0:T(8,128)S(1)}, f32[64,4,128]{2,1,0:T(4,128)S(1)}) custom-call(bf16[256,3072]{1,0:T(8,128)(2,1)S(1)} %bitcast.11, bf16[1024,3072]{1,0:T(8,128)(2,1)S(1)} %get-tuple-element.39.refs_1_.refs_2_.refs_4_.table, bf16[1024,3072]{1,0:T(8,128)(2,1)S(1)} %collective-permute-done.refs_2_.refs_3_.refs_5_.table), custom_call_target="tpu_custom_call" | custom-call | tf_op jit(solution)/shard_map/pallas_call | solution.py:45
  40.3 14.3 %all_to_all.36.refs_1_ = f32[64,4,128]{2,1,0:T(4,128)S(1)} all-to-all(f32[64,4,128]{2,1,0:T(4,128)S(1)} %get-tuple-element.41), channel_id=1, replica_groups=mesh['zh'=2,'y'=4,'x'=4,'zl'=2,'c'=2] {'zh','y','x','zl'}, dimensions={0} | all-to-all | bytes 262144 | tf_op jit(solution)/shard_map/all_to_all | solution.py:29
  54.6 3.6 %shard_map.96 = (bf16[2048,256]{1,0:T(8,128)(2,1)S(1)}, bf16[64,4,3072]{2,1,0:T(4,128)(2,1)S(1)}, f32[8,256]{1,0:T(8,128)S(1)}) custom-call(f32[2048,256]{1,0:T(8,128)S(1)} %get-tuple-element.40.refs_0_.logits, f32[64,4,128]{2,1,0:T(4,128)S(1)} %all_to_all.36.refs_1_, bf16[1024,3072]{1,0:T(8,128)(2,1)S(1)} %get-tuple-element.39.refs_1_.refs_2_.refs_4_.table, ...), custom_call_target="tpu_custom_call" | custom-call | tf_op jit(solution)/shard_map/pallas_call | solution.py:45
  58.2 0.0 copy-start
  58.2 25.6 %all_to_all.37.parts = bf16[64,4,3072]{2,1,0:T(4,128)(2,1)S(1)} all-to-all(bf16[64,4,3072]{2,1,0:T(4,128)(2,1)S(1)} %get-tuple-element.42), channel_id=1, replica_groups=mesh['zh'=2,'y'=4,'x'=4,'zl'=2,'c'=2] {'zh','y','x','zl'}, dimensions={0} | all-to-all | bytes 3145728 | tf_op jit(solution)/shard_map/all_to_all | solution.py:29
  83.8 0.4 shard_map.97
  84.2 28.2 %all_to_all.38.refs_0_ = bf16[64,4,3072]{2,1,0:T(4,128)(2,1)S(1)} all-to-all(bf16[64,4,3072]{2,1,0:T(4,128)(2,1)S(1)} %get-tuple-element.44), channel_id=1, replica_groups=mesh['zh'=2,'y'=4,'x'=4,'zl'=2,'c'=2] {'zh','y','x','zl'}, dimensions={0} | all-to-all | bytes 3145728 | tf_op jit(solution)/shard_map/all_to_all | solution.py:29
  112.5 3.0 %collective-permute-start.2 = (bf16[256,3072]{1,0:T(8,128)(2,1)S(1)}, bf16[256,3072]{1,0:T(8,128)(2,1)S(1)}, u32[]{:S(2)}, u32[]{:S(2)}) collective-permute-start(bf16[256,3072]{1,0:T(8,128)(2,1)S(1)} %bitcast.12), channel_id=1, source_target_pairs={{0,1},{1,0},{2,3},{3,2},{4,5},{5,4},{6,7},{7,6},{8,9},{9,8},{10,11... | collective-permute-start | bytes 4718600 | tf_op jit(solution)/shard_map/ppermute | solution.py:25
  115.5 0.3 collective-permute-start.1
  115.8 4.0 %shard_map.98 = (f32[2048,256]{1,0:T(8,128)S(1)}, f32[64,4,128]{2,1,0:T(4,128)S(1)}, bf16[256,3072]{1,0:T(8,128)(2,1)S(1)}) custom-call(bf16[64,4,3072]{2,1,0:T(4,128)(2,1)S(1)} %all_to_all.38.refs_0_, bf16[1024,3072]{1,0:T(8,128)(2,1)S(1)} %get-tuple-element.39.refs_1_.refs_2_.refs_4_.table, ...), custom_call_target="tpu_custom_call" | custom-call | tf_op jit(solution)/shard_map/pallas_call | solution.py:45
  119.8 0.0 collective-permute-done.2.refs_11_
  119.8 14.3 %all_to_all.39.refs_2_ = f32[64,4,128]{2,1,0:T(4,128)S(1)} all-to-all(f32[64,4,128]{2,1,0:T(4,128)S(1)} %get-tuple-element.51), channel_id=1, replica_groups=mesh['zh'=2,'y'=4,'x'=4,'zl'=2,'c'=2] {'zh','y','x','zl'}, dimensions={0} | all-to-all | bytes 262144 | tf_op jit(solution)/shard_map/all_to_all | solution.py:29
  134.2 4.6 %shard_map.99 = (bf16[2048,256]{1,0:T(8,128)(2,1)S(1)}, bf16[64,4,3072]{2,1,0:T(4,128)(2,1)S(1)}) custom-call(s32[5]{0:T(128)S(1)} %stack.23.place.refs_0_, f32[2048,256]{1,0:T(8,128)S(1)} %get-tuple-element.47.refs_1_, f32[64,4,128]{2,1,0:T(4,128)S(1)} %all_to_all.39.refs_2_, s32[8,256]{1,0:T(8,128)S(1)} %get-tuple-element.52.refs_3_.aux, ...), custom_call_target="tpu_custom_call" | custom-call | tf_op jit(solution)/shard_map/pallas_call | solution.py:45
  138.8 26.2 %all_to_all.40.parts = bf16[64,4,3072]{2,1,0:T(4,128)(2,1)S(1)} all-to-all(bf16[64,4,3072]{2,1,0:T(4,128)(2,1)S(1)} %get-tuple-element.53), channel_id=1, replica_groups=mesh['zh'=2,'y'=4,'x'=4,'zl'=2,'c'=2] {'zh','y','x','zl'}, dimensions={0} | all-to-all | bytes 3145728 | tf_op jit(solution)/shard_map/all_to_all | solution.py:29
  165.0 0.5 shard_map.100
  165.6 27.1 %all_to_all.41.pieces = bf16[64,4,3200]{2,1,0:T(4,128)(2,1)S(1)} all-to-all(bf16[64,4,3200]{2,1,0:T(4,128)(2,1)S(1)} %shard_map.100), channel_id=1, replica_groups=mesh['zh'=2,'y'=4,'x'=4,'zl'=2,'c'=2] {'zh','y','x','zl'}, dimensions={0} | all-to-all | bytes 3276800 | tf_op jit(solution)/shard_map/all_to_all | solution.py:29
  192.7 1.5 shard_map.101
  194.3 3.9 %collective-permute-start.4 = (bf16[256,3200]{1,0:T(8,128)(2,1)S(1)}, bf16[256,3200]{1,0:T(8,128)(2,1)S(1)}, u32[]{:S(2)}, u32[]{:S(2)}) collective-permute-start(bf16[256,3200]{1,0:T(8,128)(2,1)S(1)} %get-tuple-element.62.hidden.refs_8_.refs_12_), channel_id=1, source_target_pairs={{0,1},{1,0},{2,3},{3,2},{4,5},{5,4},{6,7},{7,6},{8,9},{9,8},{10,11... | collective-permute-start | bytes 4915208 | tf_op jit(solution)/shard_map/ppermute | solution.py:25
  198.2 0.1 collective-permute-start.6
  198.3 0.7 collective-permute-start.3
  199.1 2.7 %shard_map.103 = bf16[1024,256]{1,0:T(8,128)(2,1)S(1)} custom-call(s32[5]{0:T(128)S(1)} %stack.23.place.refs_0_, bf16[256,3200]{1,0:T(8,128)(2,1)S(1)} %get-tuple-element.62.hidden.refs_8_.refs_12_, f32[2048,256]{1,0:T(8,128)S(1)} %get-tuple-element.40.refs_0_.logits, f32[8,256]{1,0:T(8,128)S(1)} %get-tuple-element.63.rows, ...), custom_call_target="tpu_custom_call" | custom-call | tf_op jit(solution)/shard_map/pallas_call | solution.py:45
  201.7 0.2 collective-permute-start.5
  201.9 0.4 collective-permute-start.7
  202.3 0.0 collective-permute-done.4.refs_10_.refs_13_
  202.3 2.7 %shard_map.102.refs_3_ = bf16[1024,256]{1,0:T(8,128)(2,1)S(1)} custom-call(s32[5]{0:T(128)S(1)} %stack.23.place.refs_0_, bf16[256,3200]{1,0:T(8,128)(2,1)S(1)} %get-tuple-element.62.hidden.refs_8_.refs_12_, f32[2048,256]{1,0:T(8,128)S(1)} %get-tuple-element.40.refs_0_.logits, f32[8,256]{1,0:T(8,128)S(1)} %get-tuple-element.63.rows, ...), custom_call_target="tpu_custom_call" | custom-call | tf_op jit(solution)/shard_map/pallas_call | solution.py:45
  205.0 0.1 collective-permute-done.7.refs_15_
  205.1 12.9 %shard_map.104 = (f32[1024,3072]{1,0:T(8,128)}, bf16[64,3072]{1,0:T(8,128)(2,1)}, f32[1,3072]{1,0:T(1,128)}) custom-call(s32[5]{0:T(128)S(1)} %stack.23.place.refs_0_, bf16[2048,256]{1,0:T(8,128)(2,1)S(1)} %get-tuple-element.59.refs_0_, bf16[1024,256]{1,0:T(8,128)(2,1)S(1)} %collective-permute-done.3.refs_1_, ...), custom_call_target="tpu_custom_call" | custom-call | tf_op jit(solution)/shard_map/pallas_call | solution.py:404
  (7 shorter events, 0.1 us)
Async XLA Ops:
  4.4 31.8 %collective-permute-start = (bf16[1024,3072]{1,0:T(8,128)(2,1)S(1)}, bf16[1024,3072]{1,0:T(8,128)(2,1)S(1)}, u32[]{:S(2)}, u32[]{:S(2)}) collective-permute-start(bf16[1024,3072]{1,0:T(8,128)(2,1)S(1)} %get-tuple-element.39.refs_1_.refs_2_.refs_4_.table), channel_id=1, source_target_pairs={{0,1},{1,0},{2,3},{3,2},{4,5},{5,4},{6,7},{7,6},{8,9},{9,8},{10,11... | collective-permute-start | bytes 18874376 | tf_op jit(solution)/shard_map/ppermute | solution.py:25
  58.2 25.6 %copy-start = (f32[3072]{0:T(1024)S(1)}, f32[3072]{0:T(1024)}, u32[]{:S(2)}) copy-start(f32[3072]{0:T(1024)} %param.9) | copy-start | bytes 36868
  112.5 7.4 %collective-permute-start.2 = (bf16[256,3072]{1,0:T(8,128)(2,1)S(1)}, bf16[256,3072]{1,0:T(8,128)(2,1)S(1)}, u32[]{:S(2)}, u32[]{:S(2)}) collective-permute-start(bf16[256,3072]{1,0:T(8,128)(2,1)S(1)} %bitcast.12), channel_id=1, source_target_pairs={{0,1},{1,0},{2,3},{3,2},{4,5},{5,4},{6,7},{7,6},{8,9},{9,8},{10,11... | collective-permute-start | bytes 4718600 | tf_op jit(solution)/shard_map/ppermute | solution.py:25
  115.5 4.3 %collective-permute-start.1 = (bf16[1024,256]{1,0:T(8,128)(2,1)S(1)}, bf16[1024,256]{1,0:T(8,128)(2,1)S(1)}, u32[]{:S(2)}, u32[]{:S(2)}) collective-permute-start(bf16[1024,256]{1,0:T(8,128)(2,1)S(1)} %slice.6), channel_id=1, source_target_pairs={{0,1},{1,0},{2,3},{3,2},{4,5},{5,4},{6,7},{7,6},{8,9},{9,8},{10,11... | collective-permute-start | bytes 1572872 | tf_op jit(solution)/shard_map/ppermute | solution.py:25
  194.3 8.0 %collective-permute-start.4 = (bf16[256,3200]{1,0:T(8,128)(2,1)S(1)}, bf16[256,3200]{1,0:T(8,128)(2,1)S(1)}, u32[]{:S(2)}, u32[]{:S(2)}) collective-permute-start(bf16[256,3200]{1,0:T(8,128)(2,1)S(1)} %get-tuple-element.62.hidden.refs_8_.refs_12_), channel_id=1, source_target_pairs={{0,1},{1,0},{2,3},{3,2},{4,5},{5,4},{6,7},{7,6},{8,9},{9,8},{10,11... | collective-permute-start | bytes 4915208 | tf_op jit(solution)/shard_map/ppermute | solution.py:25
  198.2 6.9 %collective-permute-start.6 = (bf16[256,3072]{1,0:T(8,128)(2,1)S(1)}, bf16[256,3072]{1,0:T(8,128)(2,1)S(1)}, u32[]{:S(2)}, u32[]{:S(2)}) collective-permute-start(bf16[256,3072]{1,0:T(8,128)(2,1)S(1)} %get-tuple-element.61.next_input.refs_6_), channel_id=1, source_target_pairs={{0,1},{1,0},{2,3},{3,2},{4,5},{5,4},{6,7},{7,6},{8,9},{9,8},{10,11... | collective-permute-start | bytes 4718600 | tf_op jit(solution)/shard_map/ppermute | solution.py:25
  198.3 6.8 %collective-permute-start.3 = (bf16[1024,256]{1,0:T(8,128)(2,1)S(1)}, bf16[1024,256]{1,0:T(8,128)(2,1)S(1)}, u32[]{:S(2)}, u32[]{:S(2)}) collective-permute-start(bf16[1024,256]{1,0:T(8,128)(2,1)S(1)} %slice.7), channel_id=1, source_target_pairs={{0,1},{1,0},{2,3},{3,2},{4,5},{5,4},{6,7},{7,6},{8,9},{9,8},{10,11... | collective-permute-start | bytes 1572872 | tf_op jit(solution)/shard_map/ppermute | solution.py:25
  201.7 3.4 %collective-permute-start.5 = (bf16[1024,256]{1,0:T(8,128)(2,1)S(1)}, bf16[1024,256]{1,0:T(8,128)(2,1)S(1)}, u32[]{:S(2)}, u32[]{:S(2)}) collective-permute-start(bf16[1024,256]{1,0:T(8,128)(2,1)S(1)} %shard_map.103), channel_id=1, source_target_pairs={{0,1},{1,0},{2,3},{3,2},{4,5},{5,4},{6,7},{7,6},{8,9},{9,8},{10,11... | collective-permute-start | bytes 1572872 | tf_op jit(solution)/shard_map/ppermute | solution.py:25
  201.9 3.2 %collective-permute-start.7 = (f32[1,3072]{1,0:T(1,128)S(1)}, f32[1,3072]{1,0:T(1,128)S(1)}, u32[]{:S(2)}, u32[]{:S(2)}) collective-permute-start(f32[1,3072]{1,0:T(1,128)S(1)} %get-tuple-element.69.refs_14_), channel_id=1, source_target_pairs={{0,1},{1,0},{2,3},{3,2},{4,5},{5,4},{6,7},{7,6},{8,9},{9,8},{10,11... | collective-permute-start | bytes 36872 | tf_op jit(solution)/shard_map/ppermute | solution.py:25
